TPU v7x, 256 devices: a whole 4x4x8 slice. The times are simulated.
256 devices in a mesh: gx: 16 (over z, core), gy: 16 (over y, x).
Axes of the slice: x: 4, y: 4, z: 8, core: 2. Of those that a mesh axis runs over, the one named last changes fastest.
Arguments:
- embeddings: bfloat16 [262144, 4096], P(('gx', 'gy')), may hold values from -100 to 100
- sketch: bfloat16 [4096, 256], replicated, may hold values from -0.09375 to 0.09375
Outputs:
- basis: bfloat16 [262144, 256], P(('gx', 'gy'))
- factor: float32 [256, 256], replicated
- projection: float32 [256, 4096], P('gx', 'gy')
All inputs are finite; a program needn't handle non-finite values.
Results may differ from a plain program's by a relative error of at most 0.0013.
Values sent between devices are 32-bit elements; how exact they have to be, the bound alone decides.
No kernel may reach another device: no remote copies, remote signals or barrier semaphores. Data moves between devices by JAX's collectives and lax.ppermute only.
A program may use at most 128 MiB of HBM per device.

v0:
```python
import functools

import jax
import jax.numpy as jnp
from jax import lax
from jax.experimental import pallas as pl
from jax.experimental.pallas import tpu as pltpu
from jax.sharding import PartitionSpec as P

HIGH = lax.Precision.HIGHEST
F32 = jnp.float32
BF16 = jnp.bfloat16
LIMIT = 60 * 1024 * 1024


def dot(left, right, left_dim=1, right_dim=0, precision=HIGH):
    return lax.dot_general(
        left, right, (((left_dim,), (right_dim,)), ((), ())), precision=precision, preferred_element_type=F32
    )


def square(size):
    row = lax.broadcasted_iota(jnp.int32, (size, size), 0)
    return row, lax.broadcasted_iota(jnp.int32, (size, size), 1)


CHUNKS = 8
SIDE = 4


def mul(left, right):
    return jnp.dot(left, right, preferred_element_type=F32)


def front_kernel(
    where_ref, rows_hbm, sketch_hbm, sketched_hbm, piece_ref, piece_away_ref, away_send, away_keep, send, keep,
    rows, sketch, sketched, split, blocks, row_sems, sketch_sems, sketched_sem, away_sems, own_sems, *, scale,
):
    depth = rows.shape[1] // CHUNKS
    rank = sketched.shape[1]
    half, width = blocks.shape[2:]
    core = where_ref[0]
    copies = []
    for c in range(CHUNKS):
        part = pl.ds(c * depth, depth)
        pair = (
            pltpu.make_async_copy(sketch_hbm.at[part], sketch.at[part], sketch_sems.at[c]),
            pltpu.make_async_copy(rows_hbm.at[:, part], rows.at[:, part], row_sems.at[c]),
        )
        for copy in pair:
            copy.start()
        copies.append(pair)
    for c in range(CHUNKS):
        for copy in copies[c]:
            copy.wait()
        part = slice(c * depth, (c + 1) * depth)
        term = mul(rows[:, part], sketch[part, :])
        sketched[...] = term if c == 0 else sketched[...] + term
    sketched_copy = pltpu.make_async_copy(sketched, sketched_hbm, sketched_sem)
    sketched_copy.start()

    value = sketched[...]
    high = value.astype(BF16)
    rest = value - high.astype(F32)
    low = rest.astype(BF16)
    last = (rest - low.astype(F32)).astype(BF16)
    turned_high, turned_low = high.T, low.T
    split[:rank, :] = turned_high
    split[rank:, :] = turned_low
    even = mul(turned_high, high) + mul(turned_low, low)
    cross = mul(turned_high, low) + mul(turned_high, last)
    gram = (even + (cross + cross.T)) * scale
    row, col = square(half)
    end = gram[half:, half:]
    diagonal = jnp.sum(jnp.where(row == col, end, 0.0), axis=0, keepdims=True)
    corner = jnp.concatenate([gram[:half, half:], jnp.zeros((8, half), F32)])
    mixed = jnp.concatenate(
        [jnp.where(row <= col, gram[:half, :half], end), jnp.broadcast_to(diagonal, (8, half))]
    )
    piece_ref[...] = jnp.where(core == 0, corner, mixed)
    piece_away_ref[...] = jnp.where(core == 0, mixed, corner)

    outs = []
    for y in range(SIDE):
        for x in range(SIDE):
            slot = y * SIDE + x
            both = mul(split[...], rows[:, slot * width : (slot + 1) * width])
            both = both[:rank] + both[rank:]
            blocks[0, slot] = both[:half]
            blocks[1, slot] = both[half:]
            for which, bit, refs, sems in (
                (1 - core, where_ref[2], (away_send, away_keep), away_sems),
                (core, where_ref[1], (send, keep), own_sems),
            ):
                outer, inner = jnp.where(which == 0, x, y), jnp.where(which == 0, y, x)
                stays = outer % 2 == bit
                for ref, wanted in zip(refs, (jnp.logical_not(stays), stays)):
                    to = ref.at[outer // 2, inner]
                    copy = pltpu.make_async_copy(blocks.at[which, slot], to, sems.at[slot])
                    pl.when(wanted)(copy.start)
                    outs.append((wanted, copy))
    for wanted, copy in outs:
        pl.when(wanted)(copy.wait)
    sketched_copy.wait()


def front(where, embeddings, sketch, scale):
    count, width = embeddings.shape
    rank = sketch.shape[1]
    half = rank // 2
    hbm = pl.BlockSpec(memory_space=pl.ANY)
    vmem = pl.BlockSpec(memory_space=pltpu.VMEM)
    piece = jax.ShapeDtypeStruct((half + 8, half), F32)
    term = jax.ShapeDtypeStruct((SIDE // 2, SIDE, half, width // SIDE**2), F32)
    return pl.pallas_call(
        functools.partial(front_kernel, scale=scale),
        in_specs=[pl.BlockSpec(memory_space=pltpu.SMEM), hbm, hbm],
        out_specs=[hbm, vmem, vmem, hbm, hbm, hbm, hbm],
        out_shape=[jax.ShapeDtypeStruct((count, rank), F32), piece, piece, term, term, term, term],
        scratch_shapes=[
            pltpu.VMEM((count, width), BF16),
            pltpu.VMEM((width, rank), BF16),
            pltpu.VMEM((count, rank), F32),
            pltpu.VMEM((2 * rank, count), BF16),
            pltpu.VMEM((2, SIDE**2, half, width // SIDE**2), F32),
            pltpu.SemaphoreType.DMA((CHUNKS,)),
            pltpu.SemaphoreType.DMA((CHUNKS,)),
            pltpu.SemaphoreType.DMA,
            pltpu.SemaphoreType.DMA((SIDE**2,)),
            pltpu.SemaphoreType.DMA((SIDE**2,)),
        ],
        compiler_params=pltpu.CompilerParams(vmem_limit_bytes=LIMIT),
        cost_estimate=pl.CostEstimate(flops=6 * count * width * rank, bytes_accessed=2**24, transcendentals=0),
        name="front",
    )(where, embeddings, sketch)


def eliminate(pair, size):
    index = lax.broadcasted_iota(jnp.int32, (size, 1), 0)
    lanes = pair.shape[1]
    for j in range(0, size, 8):
        rows = [pair[j + p : j + p + 1, :] for p in range(8)]
        a = {
            (p, q): jnp.broadcast_to(rows[p][:, j + q : j + q + 1], (1, lanes))
            for p in range(8)
            for q in range(p, 8)
        }
        done, steps = [], []
        for s in range(0, 8, 2):
            aa, ab, bb = a[s, s], a[s, s + 1], a[s + 1, s + 1]
            inverse = 1.0 / (aa * bb - ab * ab)
            u, v = rows[s], rows[s + 1]
            top = (bb * u - ab * v) * inverse
            low = (aa * v - ab * u) * inverse
            done += [u, v - (ab / aa) * u]
            cross = {
                q: (
                    (bb * a[s, q] - ab * a[s + 1, q]) * inverse,
                    (aa * a[s + 1, q] - ab * a[s, q]) * inverse,
                )
                for q in range(s + 2, 8)
            }
            for p in range(s + 2, 8):
                rows[p] = rows[p] - (a[s, p] * top + a[s + 1, p] * low)
                for q in range(p, 8):
                    a[p, q] = a[p, q] - (a[s, p] * cross[q][0] + a[s + 1, p] * cross[q][1])
            steps.append((top, low, cross))
        weight = {}
        for s in (6, 4, 2, 0):
            top, low, cross = steps[s // 2]
            for q in range(s + 2, 8):
                top = top - cross[q][0] * weight[q]
                low = low - cross[q][1] * weight[q]
            weight[s], weight[s + 1] = top, low
        if j + 8 == size:
            return jnp.concatenate([pair[:j]] + done, axis=0)
        below = index > j + 7
        total = None
        for p in range(8):
            part = jnp.where(below, pair[:, j + p : j + p + 1], 0.0) * weight[p]
            total = part if total is None else total + part
        rest = pair - total
        pair = jnp.concatenate(([rest[:j]] if j else []) + done + [rest[j + 8 :]], axis=0)
    return pair


def step_blocks(work, upper_ref, blocks, block):
    size = work.shape[0]
    row, col = square(block)
    identity = (row == col).astype(F32)
    for k in blocks:
        lo, hi = k * block, (k + 1) * block
        pair = eliminate(jnp.concatenate([work[lo:hi, lo:hi], identity], axis=1), block)
        diagonal = jnp.sum(jnp.where(row == col, pair[:, :block], 0.0), axis=1, keepdims=True)
        pair = pair * (1.0 / jnp.sqrt(diagonal))
        small = pair[:, block:]
        upper_ref[lo:hi, :] = jnp.where(row <= col, pair[:, :block], 0.0)
        wide = dot(small, work[lo:hi, :])
        left = [wide[:, :lo]] if lo else []
        right = [wide[:, hi:]] if hi < size else []
        wide = jnp.concatenate(left + [small] + right, axis=1)
        if hi < size:
            tall = dot(work[hi:, lo:hi], small, 1, 1)
            lane = lax.broadcasted_iota(jnp.int32, (size - hi, size), 1)
            old = jnp.where((lane >= lo) & (lane < hi), 0.0, work[hi:, :])
            work[hi:, :] = old - dot(tall, wide)
        work[lo:hi, :] = wide


def first_kernel(corner_ref, mixed_ref, work, upper_ref, scales_ref, *, block):
    size = work.shape[0]
    half = size // 2
    row, col = square(half)
    eye = row == col
    corner, mixed = corner_ref[:half, :], mixed_ref[:half, :]
    turned = mixed.T
    first = jnp.where(row <= col, mixed, turned)
    last = jnp.where(eye, mixed_ref[half : half + 1, :], jnp.where(row > col, mixed, turned))

    def scales(matrix):
        picked = jnp.where(eye, matrix, 0.0)
        across = jnp.sqrt(jnp.sum(picked, axis=0, keepdims=True))
        down = jnp.sqrt(jnp.sum(picked, axis=1, keepdims=True))
        return across, 1.0 / across, 1.0 / down

    root_a, lane_a, sub_a = scales(first)
    root_b, lane_b, sub_b = scales(last)
    scales_ref[0:1, :] = jnp.concatenate([root_a, root_b], axis=1)
    scales_ref[1:2, :] = jnp.concatenate([lane_a, lane_b], axis=1)
    work[:half, :half] = jnp.where(eye, 1.0, first * sub_a * lane_a)
    work[half:, half:] = jnp.where(eye, 1.0, last * sub_b * lane_b)
    middle = corner * sub_a * lane_b
    work[:half, half:] = middle
    work[half:, :half] = middle.T
    step_blocks(work, upper_ref, range(half // block), block)


def second_kernel(state_ref, upper_ref, scales_ref, factor_ref, inverse_ref, work, upper, *, block):
    size = work.shape[0]
    half = size // 2
    work[...] = state_ref[...]
    upper[:half, :] = upper_ref[:half, :]
    step_blocks(work, upper, range(half // block, size // block), block)
    lane = lax.broadcasted_iota(jnp.int32, (block, size), 1)
    root, back = scales_ref[0:1, :], scales_ref[1:2, :]
    for k in range(size // block):
        lo, hi = k * block, (k + 1) * block
        value = work[lo:hi, :]
        inverse_ref[lo:hi, :] = jnp.where(lane < hi, value, 0.0) * back
        factor_ref[lo:hi, :] = jnp.where(lane >= hi, value, 0.0) * root
        factor_ref[lo:hi, lo:hi] = upper[lo:hi, :] * root[:, lo:hi]


SMALL = 12 * 1024 * 1024


def estimate(microseconds):
    return pl.CostEstimate(flops=microseconds * 2**30, bytes_accessed=2**20, transcendentals=0)


def factorize_first(corner, mixed, size, block):
    return pl.pallas_call(
        functools.partial(first_kernel, block=block),
        out_shape=[
            jax.ShapeDtypeStruct((size, size), F32),
            jax.ShapeDtypeStruct((size, block), F32),
            jax.ShapeDtypeStruct((8, size), F32),
        ],
        compiler_params=pltpu.CompilerParams(vmem_limit_bytes=SMALL),
        cost_estimate=estimate(6),
        name="factorize_first",
    )(corner, mixed)


def factorize_second(state, upper, scales, block):
    size = state.shape[0]
    return pl.pallas_call(
        functools.partial(second_kernel, block=block),
        out_shape=[jax.ShapeDtypeStruct((size, size), F32)] * 2,
        scratch_shapes=[pltpu.VMEM((size, size), F32), pltpu.VMEM((size, block), F32)],
        compiler_params=pltpu.CompilerParams(vmem_limit_bytes=SMALL),
        cost_estimate=estimate(6),
        name="factorize_second",
    )(state, upper, scales)


def basis_kernel(sketched_ref, inverse_ref, basis_ref):
    basis_ref[...] = dot(sketched_ref[...], inverse_ref[...], 1, 1).astype(BF16)


def basis_of(sketched, inverse):
    return pl.pallas_call(
        basis_kernel,
        out_shape=jax.ShapeDtypeStruct(sketched.shape, BF16),
        compiler_params=pltpu.CompilerParams(vmem_limit_bytes=SMALL),
        cost_estimate=estimate(2),
        name="basis",
    )(sketched, inverse)


def trade(value, masks):
    across, along = lax.axis_size("gx"), lax.axis_size("gy")
    pairs = []
    for i in range(across):
        mask_x, mask_y = masks[i % 2]
        for j in range(along):
            pairs.append((i * along + j, (i ^ mask_x) * along + (j ^ mask_y)))
    return lax.ppermute(value, ("gx", "gy"), pairs)


X1, X2, Y1, Y2 = (0, 1), (0, 2), (0, 4), (0, 8)
Z1, Z2, Z7 = (2, 0), (4, 0), (14, 0)
CORE = ((1, 0), (1, 0))


X3, Y3 = (0, 3), (0, 12)


def halves(value, bit, dim):
    keep = lax.dynamic_index_in_dim(value, bit, dim, keepdims=False)
    return keep, lax.dynamic_index_in_dim(value, 1 - bit, dim, keepdims=False)


def after(value, *others):
    return lax.optimization_barrier((value, *others))[0]


def order(core, mine, other):
    return jnp.where(core == 0, jnp.stack([mine, other]), jnp.stack([other, mine]))


def body(embeddings, sketch):
    total_rows = embeddings.shape[0] * lax.axis_size("gx") * lax.axis_size("gy")
    rank = sketch.shape[1]
    core = lax.axis_index("gx") % 2
    place = lax.axis_index("gy")
    x, y = place % SIDE, place // SIDE
    outer, inner = jnp.where(core == 0, x, y), jnp.where(core == 0, y, x)
    where = jnp.stack([core, outer % 2, inner % 2]).astype(jnp.int32)
    sketched, piece, piece_away, *terms = front(where, embeddings, sketch, 1.0 / total_rows)
    away_send, away_keep, send, keep = terms
    away_send = trade(away_send, CORE)
    away_keep = trade(away_keep, CORE)

    piece = piece + trade(piece_away, CORE)
    sums = [piece]
    for masks in ((Z1, Z7), (Z2, Z2), (Z7, Z1), (X1, Y1), (X3, Y3), (Y1, X1), (Y3, X3)):
        sums.append(sums[-1] + trade(sums[-1], masks))
    piece = sums[-1]
    other = trade(piece, CORE)
    corner, mixed = jnp.where(core == 0, piece, other), jnp.where(core == 0, other, piece)

    send = after(send + away_send, sums[0])
    got = jnp.stack([trade(send[0], (X1, Y1)), trade(send[1], (X3, Y3))])
    term = (keep + away_keep) + got
    half, width = term.shape[2:]
    keep, send = halves(term.reshape(2, 2, 2, half, width), inner % 2, 2)
    term = keep + trade(after(send, sums[2]), (Y1, X1))
    keep, send = halves(term, outer // 2, 0)
    term = keep + trade(after(send, sums[4]), (X2, Y2))
    keep, send = halves(term, inner // 2, 0)
    term = keep + trade(after(send, sums[6]), (Y2, X2))
    term = after(term, sums[7])
    term = term + trade(term, (Z1, Z7))
    block = 64
    state = factorize_first(corner, mixed, rank, block)
    state = after(tuple(state), term)
    term = term + trade(term, (Z2, Z2))
    factor, inverse = factorize_second(*state, block)
    factor, inverse = after((factor, inverse), term)
    term = term + trade(term, (Z7, Z1))
    basis = basis_of(sketched, inverse)
    summed = order(core, term, trade(term, CORE)).reshape(rank, width)

    row_count = rank // lax.axis_size("gx")
    mine = lax.dynamic_slice_in_dim(inverse, lax.axis_index("gx") * row_count, row_count, 0)
    projection = dot(mine, summed) / total_rows
    return (basis, factor, projection)


def solution(mesh):
    placed = (P(("gx", "gy"), None), P())
    return jax.shard_map(
        body,
        mesh=mesh,
        in_specs=placed,
        out_specs=(P(("gx", "gy"), None), P(), P("gx", "gy")),
        check_vma=False,
    )
```

profile of v0, /device:TPU:1, one launch (start us, length us, event | category | flops | bytes accessed | tf_op | source)
XLA Modules:
  0.0 104.4 jit_solution(14920208693640078434)
XLA Ops:
  0.7 0.6 pad_add_fusion.where_ref
  1.3 15.5 %front.1 = (f32[1024,256]{1,0:T(8,128)}, f32[136,128]{1,0:T(8,128)}, f32[136,128]{1,0:T(8,128)}, f32[2,4,128,256]{3,2,1,0:T(8,128)}, f32[2,4,128,256]{3,2,1,0:T(...) custom-call(s32[3]{0:T(128)} %pad_add_fusion.where_ref, bf16[1024,4096]{1,0:T(8,128)(2,1)} %rows_hbm.1, ...), custom_call_target="tpu_custom_call" | custom-call | flops 6442450944 | bytes 16777216 | tf_op jit(solution)/shard_map/front/pallas_call | solution.py:115
  16.8 3.3 %collective-permute-start.10 = (f32[2,4,128,256]{3,2,1,0:T(8,128)}, f32[2,4,128,256]{3,2,1,0:T(8,128)S(1)}, u32[]{:S(2)}, u32[]{:S(2)}) collective-permute-start(f32[2,4,128,256]{3,2,1,0:T(8,128)} %get-tuple-element.34), channel_id=1, source_target_pairs={{0,16},{1,17},{2,18},{3,19},{4,20},{5,21},{6,22},{7,23},{8,24},{9,... | collective-permute-start | bytes 3145736 | tf_op jit(solution)/shard_map/ppermute | solution.py:308
  20.2 0.1 collective-permute-start.9
  20.3 0.4 collective-permute-start
  20.7 3.6 %collective-permute-done = f32[136,128]{1,0:T(8,128)S(1)} collective-permute-done((f32[136,128]{1,0:T(8,128)}, f32[136,128]{1,0:T(8,128)S(1)}, u32[]{:S(2)}, u32[]{:S(2)}) %collective-permute-start) | collective-permute-done | bytes 69664 | tf_op jit(solution)/shard_map/ppermute | solution.py:308
  24.2 0.9 add.99
  25.1 0.0 collective-permute-done.10
  25.2 1.4 %add.108 = f32[2,4,128,256]{3,2,1,0:T(8,128)S(1)} add(f32[2,4,128,256]{3,2,1,0:T(8,128)} %get-tuple-element.33, f32[2,4,128,256]{3,2,1,0:T(8,128)S(1)} %collective-permute-done.10) | non-fusion elementwise | flops 262144 | bytes 3145728 | tf_op jit(solution)/shard_map/add | solution.py:353
  26.5 0.1 slice_bitcast_fusion.1
  26.6 0.1 collective-permute-start.11
  26.7 1.4 %collective-permute-start.12 = (f32[4,128,256]{2,1,0:T(8,128)S(1)}, f32[4,128,256]{2,1,0:T(8,128)S(1)}, u32[]{:S(2)}, u32[]{:S(2)}) collective-permute-start(f32[4,128,256]{2,1,0:T(8,128)S(1)} %get-tuple-element.48), channel_id=1, source_target_pairs={{0,3},{1,2},{2,1},{3,0},{4,7},{5,6},{6,5},{7,4},{8,11},{9,10},{10,... | collective-permute-start | bytes 1572872 | tf_op jit(solution)/shard_map/ppermute | solution.py:308
  28.1 5.6 %collective-permute-start.1 = (f32[136,128]{1,0:T(8,128)S(1)}, f32[136,128]{1,0:T(8,128)S(1)}, u32[]{:S(2)}, u32[]{:S(2)}) collective-permute-start(f32[136,128]{1,0:T(8,128)S(1)} %add.99), channel_id=1, source_target_pairs={{0,32},{1,33},{2,34},{3,35},{4,36},{5,37},{6,38},{7,39},{8,40},{9,... | collective-permute-start | bytes 208904 | tf_op jit(solution)/shard_map/ppermute | solution.py:308
  33.7 2.7 %collective-permute-done.1 = f32[136,128]{1,0:T(8,128)S(1)} collective-permute-done((f32[136,128]{1,0:T(8,128)S(1)}, f32[136,128]{1,0:T(8,128)S(1)}, u32[]{:S(2)}, u32[]{:S(2)}) %collective-permute-start.1) | collective-permute-done | bytes 69664 | tf_op jit(solution)/shard_map/ppermute | solution.py:308
  36.5 1.2 %collective-permute-start.2 = (f32[136,128]{1,0:T(8,128)S(1)}, f32[136,128]{1,0:T(8,128)S(1)}, u32[]{:S(2)}, u32[]{:S(2)}) collective-permute-start(f32[136,128]{1,0:T(8,128)S(1)} %add.100), channel_id=1, source_target_pairs={{0,64},{1,65},{2,66},{3,67},{4,68},{5,69},{6,70},{7,71},{8,72},{9,... | collective-permute-start | bytes 208904 | tf_op jit(solution)/shard_map/ppermute | solution.py:308
  37.7 3.7 %collective-permute-done.2 = f32[136,128]{1,0:T(8,128)S(1)} collective-permute-done((f32[136,128]{1,0:T(8,128)S(1)}, f32[136,128]{1,0:T(8,128)S(1)}, u32[]{:S(2)}, u32[]{:S(2)}) %collective-permute-start.2) | collective-permute-done | bytes 69664 | tf_op jit(solution)/shard_map/ppermute | solution.py:308
  41.4 0.0 collective-permute-done.9
  41.4 0.0 collective-permute-done.11
  41.4 0.0 collective-permute-done.12
  41.4 1.4 %maximum_add_fusion = f32[2,4,128,256]{3,2,1,0:T(8,128)S(1)} fusion(f32[1,4,128,256]{3,2,1,0:T(8,128)S(1)} %bitcast.31, f32[1,4,128,256]{3,2,1,0:T(8,128)S(1)} %bitcast.30, f32[2,4,128,256]{3,2,1,0:T(8,128)} %get-tuple-element.31, f32[2,4,128,256]{3,2,1,0:T(8,128)S(1)} %collective-permute-done.9), kind=kLoop, calls=%fused_computation.1 | loop fusion | flops 786432 | bytes 4194304 | tf_op jit(solution)/shard_map/add | solution.py:355
  42.9 0.5 collective-permute-start.13
  43.4 1.2 %collective-permute-start.3 = (f32[136,128]{1,0:T(8,128)S(1)}, f32[136,128]{1,0:T(8,128)S(1)}, u32[]{:S(2)}, u32[]{:S(2)}) collective-permute-start(f32[136,128]{1,0:T(8,128)S(1)} %add.101), channel_id=1, source_target_pairs={{0,224},{1,225},{2,226},{3,227},{4,228},{5,229},{6,230},{7,231},{8... | collective-permute-start | bytes 208904 | tf_op jit(solution)/shard_map/ppermute | solution.py:308
  44.6 2.3 %collective-permute-done.3 = f32[136,128]{1,0:T(8,128)S(1)} collective-permute-done((f32[136,128]{1,0:T(8,128)S(1)}, f32[136,128]{1,0:T(8,128)S(1)}, u32[]{:S(2)}, u32[]{:S(2)}) %collective-permute-start.3) | collective-permute-done | bytes 69664 | tf_op jit(solution)/shard_map/ppermute | solution.py:308
  46.9 0.9 collective-permute-start.4
  47.8 2.3 %collective-permute-done.4 = f32[136,128]{1,0:T(8,128)S(1)} collective-permute-done((f32[136,128]{1,0:T(8,128)S(1)}, f32[136,128]{1,0:T(8,128)S(1)}, u32[]{:S(2)}, u32[]{:S(2)}) %collective-permute-start.4) | collective-permute-done | bytes 69664 | tf_op jit(solution)/shard_map/ppermute | solution.py:308
  50.1 1.4 %collective-permute-done.13 = f32[2,2,128,256]{3,2,1,0:T(8,128)S(1)} collective-permute-done((f32[2,2,128,256]{3,2,1,0:T(8,128)S(1)}, f32[2,2,128,256]{3,2,1,0:T(8,128)S(1)}, u32[]{:S(2)}, u32[]{:S(2)}) %collective-permute-start.13) | collective-permute-done | bytes 524320 | tf_op jit(solution)/shard_map/ppermute | solution.py:308
  51.5 0.1 bitcast_add_fusion
  51.6 2.3 %collective-permute-start.14 = (f32[2,128,256]{2,1,0:T(8,128)S(1)}, f32[2,128,256]{2,1,0:T(8,128)S(1)}, u32[]{:S(2)}, u32[]{:S(2)}) collective-permute-start(f32[2,128,256]{2,1,0:T(8,128)S(1)} %dynamic-slice_bitcast_fusion.1), channel_id=1, source_target_pairs={{0,2},{1,3},{2,0},{3,1},{4,6},{5,7},{6,4},{7,5},{8,10},{9,11},{10,... | collective-permute-start | bytes 786440 | tf_op jit(solution)/shard_map/ppermute | solution.py:308
  53.9 0.9 collective-permute-start.5
  54.8 4.4 %collective-permute-done.5 = f32[136,128]{1,0:T(8,128)S(1)} collective-permute-done((f32[136,128]{1,0:T(8,128)S(1)}, f32[136,128]{1,0:T(8,128)S(1)}, u32[]{:S(2)}, u32[]{:S(2)}) %collective-permute-start.5) | collective-permute-done | bytes 69664 | tf_op jit(solution)/shard_map/ppermute | solution.py:308
  59.2 0.3 collective-permute-start.6
  59.5 3.6 %collective-permute-done.6 = f32[136,128]{1,0:T(8,128)S(1)} collective-permute-done((f32[136,128]{1,0:T(8,128)S(1)}, f32[136,128]{1,0:T(8,128)S(1)}, u32[]{:S(2)}, u32[]{:S(2)}) %collective-permute-start.6) | collective-permute-done | bytes 69664 | tf_op jit(solution)/shard_map/ppermute | solution.py:308
  63.1 0.0 collective-permute-done.14
  63.2 1.5 %collective-permute-start.15 = (f32[128,256]{1,0:T(8,128)S(1)}, f32[128,256]{1,0:T(8,128)S(1)}, u32[]{:S(2)}, u32[]{:S(2)}) collective-permute-start(f32[128,256]{1,0:T(8,128)S(1)} %dynamic-slice_bitcast_fusion.2), channel_id=1, source_target_pairs={{0,8},{1,9},{2,10},{3,11},{4,12},{5,13},{6,14},{7,15},{8,0},{9,1},... | collective-permute-start | bytes 393224 | tf_op jit(solution)/shard_map/ppermute | solution.py:308
  64.7 1.4 %collective-permute-start.7 = (f32[136,128]{1,0:T(8,128)S(1)}, f32[136,128]{1,0:T(8,128)S(1)}, u32[]{:S(2)}, u32[]{:S(2)}) collective-permute-start(f32[136,128]{1,0:T(8,128)S(1)} %add.105), channel_id=1, source_target_pairs={{0,12},{1,13},{2,14},{3,15},{4,8},{5,9},{6,10},{7,11},{8,4},{9,5},... | collective-permute-start | bytes 208904 | tf_op jit(solution)/shard_map/ppermute | solution.py:308
  66.1 3.2 %collective-permute-done.7 = f32[136,128]{1,0:T(8,128)S(1)} collective-permute-done((f32[136,128]{1,0:T(8,128)S(1)}, f32[136,128]{1,0:T(8,128)S(1)}, u32[]{:S(2)}, u32[]{:S(2)}) %collective-permute-start.7) | collective-permute-done | bytes 69664 | tf_op jit(solution)/shard_map/ppermute | solution.py:308
  69.3 8.3 %collective-permute-start.8 = (f32[136,128]{1,0:T(8,128)S(1)}, f32[136,128]{1,0:T(8,128)S(1)}, u32[]{:S(2)}, u32[]{:S(2)}) collective-permute-start(f32[136,128]{1,0:T(8,128)S(1)} %add.106), channel_id=1, source_target_pairs={{0,16},{1,17},{2,18},{3,19},{4,20},{5,21},{6,22},{7,23},{8,24},{9,... | collective-permute-start | bytes 208904 | tf_op jit(solution)/shard_map/ppermute | solution.py:308
  77.6 0.0 collective-permute-done.15
  77.6 2.9 %collective-permute-start.16 = (f32[128,256]{1,0:T(8,128)S(1)}, f32[128,256]{1,0:T(8,128)S(1)}, u32[]{:S(2)}, u32[]{:S(2)}) collective-permute-start(f32[128,256]{1,0:T(8,128)S(1)} %bitcast_add_fusion.2), channel_id=1, source_target_pairs={{0,32},{1,33},{2,34},{3,35},{4,36},{5,37},{6,38},{7,39},{8,40},{9,... | collective-permute-start | bytes 393224 | tf_op jit(solution)/shard_map/ppermute | solution.py:308
  80.5 0.0 collective-permute-done.8
  80.5 3.7 %collective-permute-done.16 = f32[128,256]{1,0:T(8,128)S(1)} collective-permute-done((f32[128,256]{1,0:T(8,128)S(1)}, f32[128,256]{1,0:T(8,128)S(1)}, u32[]{:S(2)}, u32[]{:S(2)}) %collective-permute-start.16) | collective-permute-done | bytes 131104 | tf_op jit(solution)/shard_map/ppermute | solution.py:308
  84.3 1.7 %collective-permute-start.17 = (f32[128,256]{1,0:T(8,128)S(1)}, f32[128,256]{1,0:T(8,128)S(1)}, u32[]{:S(2)}, u32[]{:S(2)}) collective-permute-start(f32[128,256]{1,0:T(8,128)S(1)} %add.119), channel_id=1, source_target_pairs={{0,64},{1,65},{2,66},{3,67},{4,68},{5,69},{6,70},{7,71},{8,72},{9,... | collective-permute-start | bytes 393224 | tf_op jit(solution)/shard_map/ppermute | solution.py:308
  86.0 5.3 %factorize_first.1 = (f32[256,256]{1,0:T(8,128)S(1)}, f32[256,64]{1,0:T(8,128)S(1)}, f32[8,256]{1,0:T(8,128)S(1)}) custom-call(f32[136,128]{1,0:T(8,128)S(1)} %get-tuple-element.50.corner_ref, f32[136,128]{1,0:T(8,128)S(1)} %get-tuple-element.49.mixed_ref), custom_call_target="tpu_custom_call" | custom-call | flops 6442450944 | bytes 1048576 | tf_op jit(solution)/shard_map/factorize_first/pallas_call | solution.py:262
  91.3 1.0 collective-permute-done.17
  92.3 0.0 copy-start
  92.3 0.3 collective-permute-start.18
  92.6 5.0 %factorize_second.1 = (f32[256,256]{1,0:T(8,128)}, f32[256,256]{1,0:T(8,128)S(1)}) custom-call(f32[256,256]{1,0:T(8,128)S(1)} %get-tuple-element.40.state_ref, f32[256,64]{1,0:T(8,128)S(1)} %get-tuple-element.41.upper_ref, f32[8,256]{1,0:T(8,128)S(1)} %get-tuple-element.42.scales_ref), custom_call_target="tpu_custom_call" | custom-call | flops 6442450944 | bytes 1048576 | tf_op jit(solution)/shard_map/factorize_second/pallas_call | solution.py:277
  97.6 0.0 collective-permute-done.18
  97.6 4.0 %collective-permute-start.19 = (f32[128,256]{1,0:T(8,128)S(1)}, f32[128,256]{1,0:T(8,128)S(1)}, u32[]{:S(2)}, u32[]{:S(2)}) collective-permute-start(f32[128,256]{1,0:T(8,128)S(1)} %add.122), channel_id=1, source_target_pairs={{0,16},{1,17},{2,18},{3,19},{4,20},{5,21},{6,22},{7,23},{8,24},{9,... | collective-permute-start | bytes 393224 | tf_op jit(solution)/shard_map/ppermute | solution.py:308
  101.7 0.0 copy-done
  101.7 1.8 %basis.1 = bf16[1024,256]{1,0:T(8,128)(2,1)} custom-call(f32[1024,256]{1,0:T(8,128)S(1)} %copy-done, f32[256,256]{1,0:T(8,128)S(1)} %get-tuple-element.45.inverse_ref), custom_call_target="tpu_custom_call" | custom-call | flops 2147483648 | bytes 1048576 | tf_op jit(solution)/shard_map/basis/pallas_call | solution.py:292
  103.5 0.0 collective-permute-done.19
  103.5 0.8 convolution_multiply_fusion
  (17 shorter events, 0.3 us)
Async XLA Ops:
  16.8 8.3 %collective-permute-start.10 = (f32[2,4,128,256]{3,2,1,0:T(8,128)}, f32[2,4,128,256]{3,2,1,0:T(8,128)S(1)}, u32[]{:S(2)}, u32[]{:S(2)}) collective-permute-start(f32[2,4,128,256]{3,2,1,0:T(8,128)} %get-tuple-element.34), channel_id=1, source_target_pairs={{0,16},{1,17},{2,18},{3,19},{4,20},{5,21},{6,22},{7,23},{8,24},{9,... | collective-permute-start | bytes 3145736 | tf_op jit(solution)/shard_map/ppermute | solution.py:308
  20.2 21.2 %collective-permute-start.9 = (f32[2,4,128,256]{3,2,1,0:T(8,128)}, f32[2,4,128,256]{3,2,1,0:T(8,128)S(1)}, u32[]{:S(2)}, u32[]{:S(2)}) collective-permute-start(f32[2,4,128,256]{3,2,1,0:T(8,128)} %get-tuple-element.32), channel_id=1, source_target_pairs={{0,16},{1,17},{2,18},{3,19},{4,20},{5,21},{6,22},{7,23},{8,24},{9,... | collective-permute-start | bytes 3145736 | tf_op jit(solution)/shard_map/ppermute | solution.py:308
  20.3 4.0 %collective-permute-start = (f32[136,128]{1,0:T(8,128)}, f32[136,128]{1,0:T(8,128)S(1)}, u32[]{:S(2)}, u32[]{:S(2)}) collective-permute-start(f32[136,128]{1,0:T(8,128)} %get-tuple-element.27), channel_id=1, source_target_pairs={{0,16},{1,17},{2,18},{3,19},{4,20},{5,21},{6,22},{7,23},{8,24},{9,... | collective-permute-start | bytes 208904 | tf_op jit(solution)/shard_map/ppermute | solution.py:308
  26.6 14.8 %collective-permute-start.11 = (f32[4,128,256]{2,1,0:T(8,128)S(1)}, f32[4,128,256]{2,1,0:T(8,128)S(1)}, u32[]{:S(2)}, u32[]{:S(2)}) collective-permute-start(f32[4,128,256]{2,1,0:T(8,128)S(1)} %get-tuple-element.47), channel_id=1, source_target_pairs={{0,1},{1,0},{2,3},{3,2},{4,5},{5,4},{6,7},{7,6},{8,9},{9,8},{10,11... | collective-permute-start | bytes 1572872 | tf_op jit(solution)/shard_map/ppermute | solution.py:308
  26.7 14.7 %collective-permute-start.12 = (f32[4,128,256]{2,1,0:T(8,128)S(1)}, f32[4,128,256]{2,1,0:T(8,128)S(1)}, u32[]{:S(2)}, u32[]{:S(2)}) collective-permute-start(f32[4,128,256]{2,1,0:T(8,128)S(1)} %get-tuple-element.48), channel_id=1, source_target_pairs={{0,3},{1,2},{2,1},{3,0},{4,7},{5,6},{6,5},{7,4},{8,11},{9,10},{10,... | collective-permute-start | bytes 1572872 | tf_op jit(solution)/shard_map/ppermute | solution.py:308
  28.1 8.3 %collective-permute-start.1 = (f32[136,128]{1,0:T(8,128)S(1)}, f32[136,128]{1,0:T(8,128)S(1)}, u32[]{:S(2)}, u32[]{:S(2)}) collective-permute-start(f32[136,128]{1,0:T(8,128)S(1)} %add.99), channel_id=1, source_target_pairs={{0,32},{1,33},{2,34},{3,35},{4,36},{5,37},{6,38},{7,39},{8,40},{9,... | collective-permute-start | bytes 208904 | tf_op jit(solution)/shard_map/ppermute | solution.py:308
  36.5 4.9 %collective-permute-start.2 = (f32[136,128]{1,0:T(8,128)S(1)}, f32[136,128]{1,0:T(8,128)S(1)}, u32[]{:S(2)}, u32[]{:S(2)}) collective-permute-start(f32[136,128]{1,0:T(8,128)S(1)} %add.100), channel_id=1, source_target_pairs={{0,64},{1,65},{2,66},{3,67},{4,68},{5,69},{6,70},{7,71},{8,72},{9,... | collective-permute-start | bytes 208904 | tf_op jit(solution)/shard_map/ppermute | solution.py:308
  42.9 8.6 %collective-permute-start.13 = (f32[2,2,128,256]{3,2,1,0:T(8,128)S(1)}, f32[2,2,128,256]{3,2,1,0:T(8,128)S(1)}, u32[]{:S(2)}, u32[]{:S(2)}) collective-permute-start(f32[2,2,128,256]{3,2,1,0:T(8,128)S(1)} %dynamic-slice_bitcast_fusion), channel_id=1, source_target_pairs={{0,4},{1,5},{2,6},{3,7},{4,0},{5,1},{6,2},{7,3},{8,12},{9,13},{10,... | collective-permute-start | bytes 1572872 | tf_op jit(solution)/shard_map/ppermute | solution.py:308
  43.4 3.5 %collective-permute-start.3 = (f32[136,128]{1,0:T(8,128)S(1)}, f32[136,128]{1,0:T(8,128)S(1)}, u32[]{:S(2)}, u32[]{:S(2)}) collective-permute-start(f32[136,128]{1,0:T(8,128)S(1)} %add.101), channel_id=1, source_target_pairs={{0,224},{1,225},{2,226},{3,227},{4,228},{5,229},{6,230},{7,231},{8... | collective-permute-start | bytes 208904 | tf_op jit(solution)/shard_map/ppermute | solution.py:308
  46.9 3.2 %collective-permute-start.4 = (f32[136,128]{1,0:T(8,128)S(1)}, f32[136,128]{1,0:T(8,128)S(1)}, u32[]{:S(2)}, u32[]{:S(2)}) collective-permute-start(f32[136,128]{1,0:T(8,128)S(1)} %add.102), channel_id=1, source_target_pairs={{0,1},{1,0},{2,3},{3,2},{4,5},{5,4},{6,7},{7,6},{8,9},{9,8},{10,11... | collective-permute-start | bytes 208904 | tf_op jit(solution)/shard_map/ppermute | solution.py:308
  51.6 11.5 %collective-permute-start.14 = (f32[2,128,256]{2,1,0:T(8,128)S(1)}, f32[2,128,256]{2,1,0:T(8,128)S(1)}, u32[]{:S(2)}, u32[]{:S(2)}) collective-permute-start(f32[2,128,256]{2,1,0:T(8,128)S(1)} %dynamic-slice_bitcast_fusion.1), channel_id=1, source_target_pairs={{0,2},{1,3},{2,0},{3,1},{4,6},{5,7},{6,4},{7,5},{8,10},{9,11},{10,... | collective-permute-start | bytes 786440 | tf_op jit(solution)/shard_map/ppermute | solution.py:308
  53.9 5.3 %collective-permute-start.5 = (f32[136,128]{1,0:T(8,128)S(1)}, f32[136,128]{1,0:T(8,128)S(1)}, u32[]{:S(2)}, u32[]{:S(2)}) collective-permute-start(f32[136,128]{1,0:T(8,128)S(1)} %add.103), channel_id=1, source_target_pairs={{0,3},{1,2},{2,1},{3,0},{4,7},{5,6},{6,5},{7,4},{8,11},{9,10},{10,... | collective-permute-start | bytes 208904 | tf_op jit(solution)/shard_map/ppermute | solution.py:308
  59.2 3.9 %collective-permute-start.6 = (f32[136,128]{1,0:T(8,128)S(1)}, f32[136,128]{1,0:T(8,128)S(1)}, u32[]{:S(2)}, u32[]{:S(2)}) collective-permute-start(f32[136,128]{1,0:T(8,128)S(1)} %add.104), channel_id=1, source_target_pairs={{0,4},{1,5},{2,6},{3,7},{4,0},{5,1},{6,2},{7,3},{8,12},{9,13},{10,... | collective-permute-start | bytes 208904 | tf_op jit(solution)/shard_map/ppermute | solution.py:308
  63.2 14.5 %collective-permute-start.15 = (f32[128,256]{1,0:T(8,128)S(1)}, f32[128,256]{1,0:T(8,128)S(1)}, u32[]{:S(2)}, u32[]{:S(2)}) collective-permute-start(f32[128,256]{1,0:T(8,128)S(1)} %dynamic-slice_bitcast_fusion.2), channel_id=1, source_target_pairs={{0,8},{1,9},{2,10},{3,11},{4,12},{5,13},{6,14},{7,15},{8,0},{9,1},... | collective-permute-start | bytes 393224 | tf_op jit(solution)/shard_map/ppermute | solution.py:308
  64.7 4.6 %collective-permute-start.7 = (f32[136,128]{1,0:T(8,128)S(1)}, f32[136,128]{1,0:T(8,128)S(1)}, u32[]{:S(2)}, u32[]{:S(2)}) collective-permute-start(f32[136,128]{1,0:T(8,128)S(1)} %add.105), channel_id=1, source_target_pairs={{0,12},{1,13},{2,14},{3,15},{4,8},{5,9},{6,10},{7,11},{8,4},{9,5},... | collective-permute-start | bytes 208904 | tf_op jit(solution)/shard_map/ppermute | solution.py:308
  69.3 11.2 %collective-permute-start.8 = (f32[136,128]{1,0:T(8,128)S(1)}, f32[136,128]{1,0:T(8,128)S(1)}, u32[]{:S(2)}, u32[]{:S(2)}) collective-permute-start(f32[136,128]{1,0:T(8,128)S(1)} %add.106), channel_id=1, source_target_pairs={{0,16},{1,17},{2,18},{3,19},{4,20},{5,21},{6,22},{7,23},{8,24},{9,... | collective-permute-start | bytes 208904 | tf_op jit(solution)/shard_map/ppermute | solution.py:308
  77.6 6.7 %collective-permute-start.16 = (f32[128,256]{1,0:T(8,128)S(1)}, f32[128,256]{1,0:T(8,128)S(1)}, u32[]{:S(2)}, u32[]{:S(2)}) collective-permute-start(f32[128,256]{1,0:T(8,128)S(1)} %bitcast_add_fusion.2), channel_id=1, source_target_pairs={{0,32},{1,33},{2,34},{3,35},{4,36},{5,37},{6,38},{7,39},{8,40},{9,... | collective-permute-start | bytes 393224 | tf_op jit(solution)/shard_map/ppermute | solution.py:308
  84.3 8.0 %collective-permute-start.17 = (f32[128,256]{1,0:T(8,128)S(1)}, f32[128,256]{1,0:T(8,128)S(1)}, u32[]{:S(2)}, u32[]{:S(2)}) collective-permute-start(f32[128,256]{1,0:T(8,128)S(1)} %add.119), channel_id=1, source_target_pairs={{0,64},{1,65},{2,66},{3,67},{4,68},{5,69},{6,70},{7,71},{8,72},{9,... | collective-permute-start | bytes 393224 | tf_op jit(solution)/shard_map/ppermute | solution.py:308
  92.3 9.4 %copy-start = (f32[1024,256]{1,0:T(8,128)S(1)}, f32[1024,256]{1,0:T(8,128)}, u32[]{:S(2)}) copy-start(f32[1024,256]{1,0:T(8,128)} %get-tuple-element.25.sketched_ref) | copy-start | bytes 3145732
  92.3 5.3 %collective-permute-start.18 = (f32[128,256]{1,0:T(8,128)S(1)}, f32[128,256]{1,0:T(8,128)S(1)}, u32[]{:S(2)}, u32[]{:S(2)}) collective-permute-start(f32[128,256]{1,0:T(8,128)S(1)} %add.120), channel_id=1, source_target_pairs={{0,224},{1,225},{2,226},{3,227},{4,228},{5,229},{6,230},{7,231},{8... | collective-permute-start | bytes 393224 | tf_op jit(solution)/shard_map/ppermute | solution.py:308
  97.6 5.9 %collective-permute-start.19 = (f32[128,256]{1,0:T(8,128)S(1)}, f32[128,256]{1,0:T(8,128)S(1)}, u32[]{:S(2)}, u32[]{:S(2)}) collective-permute-start(f32[128,256]{1,0:T(8,128)S(1)} %add.122), channel_id=1, source_target_pairs={{0,16},{1,17},{2,18},{3,19},{4,20},{5,21},{6,22},{7,23},{8,24},{9,... | collective-permute-start | bytes 393224 | tf_op jit(solution)/shard_map/ppermute | solution.py:308
where the time goes:
time: 105 us; the launch traced here: 104 us
  starting transfers between devices  38.4 us (37%)
  waiting for transfers between devices  31.8 us (30%)
  Pallas kernels  27.6 us (26%)
  other arithmetic  4.57 us (4%)
    ppermute x20, starting transfers between devices, trade(): return lax.ppermute(value, ('gx', 'gy'), pairs)  38.4 us
    ppermute x20, waiting for transfers between devices, trade(): return lax.ppermute(value, ('gx', 'gy'), pairs)  31.8 us
    pallas_call x1, Pallas kernels, front(): pl.pallas_call(functools.partial(front_kernel, scale=scale), in_specs=[pl...  15.5 us
    pallas_call x1, Pallas kernels, factorize_first(): pl.pallas_call(functools.partial(first_kernel, block=block), out_shape=[j...  5.34 us
    pallas_call x1, Pallas kernels, factorize_second(): pl.pallas_call(functools.partial(second_kernel, block=block), out_shape=[...  4.97 us
  transfers between devices with their start and end apart: 20, of which 11 were waited for; matrix products, arithmetic and copies ran while one was open for 2% of the time, Pallas kernels for 12%

commit v1 on v0

--- a/solution.py
+++ b/solution.py
@@ -73,12 +73,13 @@
     row, col = square(half)
     end = gram[half:, half:]
     diagonal = jnp.sum(jnp.where(row == col, end, 0.0), axis=0, keepdims=True)
-    corner = jnp.concatenate([gram[:half, half:], jnp.zeros((8, half), F32)])
-    mixed = jnp.concatenate(
-        [jnp.where(row <= col, gram[:half, :half], end), jnp.broadcast_to(diagonal, (8, half))]
-    )
-    piece_ref[...] = jnp.where(core == 0, corner, mixed)
-    piece_away_ref[...] = jnp.where(core == 0, mixed, corner)
+    corner, mixed = gram[:half, half:], jnp.where(row <= col, gram[:half, :half], end)
+    upper = half // 2
+    for ref, first in ((piece_ref, core == 0), (piece_away_ref, core == 1)):
+        value = jnp.where(first, corner, mixed)
+        ref[:upper, :half] = value[:upper]
+        ref[:upper, half:] = value[upper:]
+        ref[upper:, :] = jnp.broadcast_to(jnp.concatenate([diagonal, diagonal], axis=1), (8, rank))
 
     outs = []
     for y in range(SIDE):
@@ -110,7 +111,7 @@
     half = rank // 2
     hbm = pl.BlockSpec(memory_space=pl.ANY)
     vmem = pl.BlockSpec(memory_space=pltpu.VMEM)
-    piece = jax.ShapeDtypeStruct((half + 8, half), F32)
+    piece = jax.ShapeDtypeStruct((half // 2 + 8, rank), F32)
     term = jax.ShapeDtypeStruct((SIDE // 2, SIDE, half, width // SIDE**2), F32)
     return pl.pallas_call(
         functools.partial(front_kernel, scale=scale),
@@ -212,10 +213,13 @@
     half = size // 2
     row, col = square(half)
     eye = row == col
-    corner, mixed = corner_ref[:half, :], mixed_ref[:half, :]
+    upper = half // 2
+    corner, mixed = (
+        jnp.concatenate([ref[:upper, :half], ref[:upper, half:]]) for ref in (corner_ref, mixed_ref)
+    )
     turned = mixed.T
     first = jnp.where(row <= col, mixed, turned)
-    last = jnp.where(eye, mixed_ref[half : half + 1, :], jnp.where(row > col, mixed, turned))
+    last = jnp.where(eye, mixed_ref[upper : upper + 1, :half], jnp.where(row > col, mixed, turned))
 
     def scales(matrix):
         picked = jnp.where(eye, matrix, 0.0)
@@ -313,12 +317,18 @@
 CORE = ((1, 0), (1, 0))
 
 
-X3, Y3 = (0, 3), (0, 12)
+X3, Y3, XY2 = (0, 3), (0, 12), (0, 10)
 
 
 def halves(value, bit, dim):
     keep = lax.dynamic_index_in_dim(value, bit, dim, keepdims=False)
     return keep, lax.dynamic_index_in_dim(value, 1 - bit, dim, keepdims=False)
+
+
+def trade_both(value, piece, masks):
+    flat = value.reshape(-1, piece.shape[1])
+    got = trade(jnp.concatenate([flat, piece]), masks)
+    return got[: flat.shape[0]].reshape(value.shape), got[flat.shape[0] :]
 
 
 def after(value, *others):
@@ -339,36 +349,45 @@
     where = jnp.stack([core, outer % 2, inner % 2]).astype(jnp.int32)
     sketched, piece, piece_away, *terms = front(where, embeddings, sketch, 1.0 / total_rows)
     away_send, away_keep, send, keep = terms
-    away_send = trade(away_send, CORE)
-    away_keep = trade(away_keep, CORE)
+    half, width = keep.shape[2:]
 
     piece = piece + trade(piece_away, CORE)
-    sums = [piece]
-    for masks in ((Z1, Z7), (Z2, Z2), (Z7, Z1), (X1, Y1), (X3, Y3), (Y1, X1), (Y3, X3)):
-        sums.append(sums[-1] + trade(sums[-1], masks))
-    piece = sums[-1]
+    send = send + trade(away_send, CORE)
+    keep = keep + trade(after(away_keep, piece), CORE)
+    one, piece_1 = trade_both(send[0], piece, (X1, Y1))
+    three, piece_3 = trade_both(send[1], piece, (X3, Y3))
+    piece = (piece + piece_1) + (trade(piece, (X2, Y2)) + piece_3)
+    terms = [(k + got).reshape(2, 2, half, width) for k, got in zip(keep, (one, three))]
+    parts = [halves(term, inner % 2, 1) for term in terms]
+    one, piece_1 = trade_both(parts[0][1], piece, (Y1, X1))
+    three, piece_3 = trade_both(parts[1][1], piece, (Y3, X3))
+    piece = (piece + piece_1) + (trade(piece, (Y2, X2)) + piece_3)
+    low, high = (part[0] + got for part, got in zip(parts, (one, three)))
+    outer, inner = outer // 2, inner // 2
+
+    def quarter(across, along):
+        pair = jnp.where((outer ^ across) == 1, high, low)
+        return lax.dynamic_index_in_dim(pair, inner ^ along, 0, keepdims=False)
+
+    one = trade(quarter(1, 1), (XY2, XY2))
+    two = trade(quarter(1, 0), (X2, Y2))
+    three = trade(quarter(0, 1), (Y2, X2))
+    piece = piece + trade(piece, (Z7, Z7))
+    term = (quarter(0, 0) + one) + (two + three)
+    piece = piece + trade(piece, (Z2, Z1))
+    piece = piece + trade(piece, (Z1, Z2))
+
     other = trade(piece, CORE)
     corner, mixed = jnp.where(core == 0, piece, other), jnp.where(core == 0, other, piece)
-
-    send = after(send + away_send, sums[0])
-    got = jnp.stack([trade(send[0], (X1, Y1)), trade(send[1], (X3, Y3))])
-    term = (keep + away_keep) + got
-    half, width = term.shape[2:]
-    keep, send = halves(term.reshape(2, 2, 2, half, width), inner % 2, 2)
-    term = keep + trade(after(send, sums[2]), (Y1, X1))
-    keep, send = halves(term, outer // 2, 0)
-    term = keep + trade(after(send, sums[4]), (X2, Y2))
-    keep, send = halves(term, inner // 2, 0)
-    term = keep + trade(after(send, sums[6]), (Y2, X2))
-    term = after(term, sums[7])
-    term = term + trade(term, (Z1, Z7))
     block = 64
+    term = term + trade(term, (Z1, Z2))
+    term, corner, mixed = lax.optimization_barrier((term, corner, mixed))
     state = factorize_first(corner, mixed, rank, block)
-    state = after(tuple(state), term)
-    term = term + trade(term, (Z2, Z2))
+    term = term + trade(term, (Z2, Z1))
+    term, *state = lax.optimization_barrier((term, *state))
     factor, inverse = factorize_second(*state, block)
-    factor, inverse = after((factor, inverse), term)
-    term = term + trade(term, (Z7, Z1))
+    term = term + trade(term, (Z7, Z7))
+    term, factor, inverse = lax.optimization_barrier((term, factor, inverse))
     basis = basis_of(sketched, inverse)
     summed = order(core, term, trade(term, CORE)).reshape(rank, width)
 

time: 105 us -> 97 us (0.924)
  waiting for transfers between devices: 31.8 us -> 19.8 us
  local copies, waits for them, and re-layouts: 0.16 us -> 2.46 us
  starting transfers between devices: 38.4 us -> 40.5 us
    ppermute x20, waiting for transfers between devices: 31.8 us -> 19.8 us  [trade(): return lax.ppermute(value, ('gx', 'gy'), pairs)]
    slice x0 -> x5, local copies, waits for them, and re-layouts: none -> 2.26 us  [the longest x4 2.19 us: trade_both(): return (got[:flat.shape[0]].reshape(value.shape), got[flat.shape[0]:])]
    ppermute x20, starting transfers between devices: 38.4 us -> 40.5 us  [trade(): return lax.ppermute(value, ('gx', 'gy'), pairs)]
    add x15 -> x13, other arithmetic: 3.04 us -> 2.73 us  [the longest x1 1.36 us: body(): send = send + trade(away_send, CORE)]
  transfers between devices with their start and end apart: 20 -> 20, of which waited for: 11 -> 6; matrix products, arithmetic and copies ran while one was open for 2% -> 5% of each run, Pallas kernels for 12% -> 13%
where the time goes in v1:
time: 97 us; the launch traced here: 96.7 us
  starting transfers between devices  40.5 us (42%)
  Pallas kernels  27.7 us (29%)
  waiting for transfers between devices  19.8 us (20%)
  other arithmetic  4.46 us (5%)
  local copies, waits for them, and re-layouts  2.46 us (3%)
    ppermute x20, starting transfers between devices, trade(): return lax.ppermute(value, ('gx', 'gy'), pairs)  40.5 us
    ppermute x20, waiting for transfers between devices, trade(): return lax.ppermute(value, ('gx', 'gy'), pairs)  19.8 us
    pallas_call x1, Pallas kernels, front(): pl.pallas_call(functools.partial(front_kernel, scale=scale), in_specs=[pl...  15.5 us
    pallas_call x1, Pallas kernels, factorize_first(): pl.pallas_call(functools.partial(first_kernel, block=block), out_shape=[j...  5.35 us
    pallas_call x1, Pallas kernels, factorize_second(): pl.pallas_call(functools.partial(second_kernel, block=block), out_shape=[...  4.97 us
    slice x4, local copies, waits for them, and re-layouts, trade_both(): return (got[:flat.shape[0]].reshape(value.shape), got[flat.shape[0]:])  2.19 us
  transfers between devices with their start and end apart: 20, of which 6 were waited for; matrix products, arithmetic and copies ran while one was open for 5% of the time, Pallas kernels for 13%

profile of v1, /device:TPU:1, one launch (start us, length us, event | category | flops | bytes accessed | tf_op | source)
XLA Modules:
  0.0 96.7 jit_solution(3881337439435352567)
XLA Ops:
  0.7 0.6 pad_add_fusion.where_ref
  1.3 15.5 %front.1 = (f32[1024,256]{1,0:T(8,128)}, f32[72,256]{1,0:T(8,128)}, f32[72,256]{1,0:T(8,128)}, f32[2,4,128,256]{3,2,1,0:T(8,128)}, f32[2,4,128,256]{3,2,1,0:T(8,...) custom-call(s32[3]{0:T(128)} %pad_add_fusion.where_ref, bf16[1024,4096]{1,0:T(8,128)(2,1)} %rows_hbm.1, ...), custom_call_target="tpu_custom_call" | custom-call | flops 6442450944 | bytes 16777216 | tf_op jit(solution)/shard_map/front/pallas_call | solution.py:116
  16.8 0.0 copy-start.1
  16.8 3.3 %collective-permute-start.2 = (f32[2,4,128,256]{3,2,1,0:T(8,128)}, f32[2,4,128,256]{3,2,1,0:T(8,128)S(1)}, u32[]{:S(2)}, u32[]{:S(2)}) collective-permute-start(f32[2,4,128,256]{3,2,1,0:T(8,128)} %get-tuple-element.33), channel_id=1, source_target_pairs={{0,16},{1,17},{2,18},{3,19},{4,20},{5,21},{6,22},{7,23},{8,24},{9,... | collective-permute-start | bytes 3145736 | tf_op jit(solution)/shard_map/ppermute | solution.py:312
  20.2 0.1 collective-permute-start
  20.3 2.5 %collective-permute-done = f32[72,256]{1,0:T(8,128)S(1)} collective-permute-done((f32[72,256]{1,0:T(8,128)}, f32[72,256]{1,0:T(8,128)S(1)}, u32[]{:S(2)}, u32[]{:S(2)}) %collective-permute-start) | collective-permute-done | bytes 73760 | tf_op jit(solution)/shard_map/ppermute | solution.py:312
  22.8 0.9 add.112
  23.7 0.5 collective-permute-start.1
  24.1 0.0 collective-permute-done.2
  24.1 1.4 %add.114 = f32[2,4,128,256]{3,2,1,0:T(8,128)S(1)} add(f32[2,4,128,256]{3,2,1,0:T(8,128)} %get-tuple-element.32, f32[2,4,128,256]{3,2,1,0:T(8,128)S(1)} %collective-permute-done.2) | non-fusion elementwise | flops 262144 | bytes 3145728 | tf_op jit(solution)/shard_map/add | solution.py:355
  25.5 0.1 fusion.6
  25.6 0.1 pad_maximum_fusion
  25.7 1.1 %collective-permute-start.3 = (f32[584,256]{1,0:T(8,128)S(1)}, f32[584,256]{1,0:T(8,128)}, u32[]{:S(2)}, u32[]{:S(2)}) collective-permute-start(f32[584,256]{1,0:T(8,128)S(1)} %get-tuple-element.62), channel_id=1, source_target_pairs={{0,3},{1,2},{2,1},{3,0},{4,7},{5,6},{6,5},{7,4},{8,11},{9,10},{10,... | collective-permute-start | bytes 1794056 | tf_op jit(solution)/shard_map/ppermute | solution.py:312
  26.8 0.0 collective-permute-start.4
  26.8 2.9 %collective-permute-start.5 = (f32[72,256]{1,0:T(8,128)S(1)}, f32[72,256]{1,0:T(8,128)S(1)}, u32[]{:S(2)}, u32[]{:S(2)}) collective-permute-start(f32[72,256]{1,0:T(8,128)S(1)} %add.112), channel_id=1, source_target_pairs={{0,2},{1,3},{2,0},{3,1},{4,6},{5,7},{6,4},{7,5},{8,10},{9,11},{10,... | collective-permute-start | bytes 221192 | tf_op jit(solution)/shard_map/ppermute | solution.py:312
  29.6 0.0 collective-permute-done.1
  29.6 0.0 copy-done.1
  29.6 0.1 add.113
  29.8 0.1 fusion.5
  29.9 6.3 %collective-permute-done.3 = f32[584,256]{1,0:T(8,128)} collective-permute-done((f32[584,256]{1,0:T(8,128)S(1)}, f32[584,256]{1,0:T(8,128)}, u32[]{:S(2)}, u32[]{:S(2)}) %collective-permute-start.3) | collective-permute-done | bytes 598048 | tf_op jit(solution)/shard_map/ppermute | solution.py:312
  36.2 1.1 %slice.41 = f32[512,256]{1,0:T(8,128)S(1)} slice(f32[584,256]{1,0:T(8,128)} %collective-permute-done.3), slice={[0:512], [0:256]} | slice | bytes 1048576 | tf_op jit(solution)/shard_map/slice | solution.py:331
  37.3 0.1 add.115
  37.4 0.0 collective-permute-done.4
  37.4 1.1 %slice.46 = f32[512,256]{1,0:T(8,128)S(1)} slice(f32[584,256]{1,0:T(8,128)} %collective-permute-done.4), slice={[0:512], [0:256]} | slice | bytes 1048576 | tf_op jit(solution)/shard_map/slice | solution.py:331
  38.5 0.1 copy_add_fusion
  38.6 0.0 collective-permute-done.5
  38.6 0.9 fusion.2
  39.6 1.3 %collective-permute-start.6 = (f32[328,256]{1,0:T(8,128)S(1)}, f32[328,256]{1,0:T(8,128)S(1)}, u32[]{:S(2)}, u32[]{:S(2)}) collective-permute-start(f32[328,256]{1,0:T(8,128)S(1)} %get-tuple-element.60), channel_id=1, source_target_pairs={{0,12},{1,13},{2,14},{3,15},{4,8},{5,9},{6,10},{7,11},{8,4},{9,5},... | collective-permute-start | bytes 1007624 | tf_op jit(solution)/shard_map/ppermute | solution.py:312
  40.9 0.0 collective-permute-start.7
  40.9 2.8 %collective-permute-start.12 = (f32[72,256]{1,0:T(8,128)S(1)}, f32[72,256]{1,0:T(8,128)S(1)}, u32[]{:S(2)}, u32[]{:S(2)}) collective-permute-start(f32[72,256]{1,0:T(8,128)S(1)} %fusion.2), channel_id=1, source_target_pairs={{0,8},{1,9},{2,10},{3,11},{4,12},{5,13},{6,14},{7,15},{8,0},{9,1},... | collective-permute-start | bytes 221192 | tf_op jit(solution)/shard_map/ppermute | solution.py:312
  43.7 5.3 %collective-permute-done.12 = f32[72,256]{1,0:T(8,128)S(1)} collective-permute-done((f32[72,256]{1,0:T(8,128)S(1)}, f32[72,256]{1,0:T(8,128)S(1)}, u32[]{:S(2)}, u32[]{:S(2)}) %collective-permute-start.12) | collective-permute-done | bytes 73760 | tf_op jit(solution)/shard_map/ppermute | solution.py:312
  49.0 0.0 collective-permute-done.6
  49.0 0.0 collective-permute-done.7
  49.1 4.3 %collective-permute-start.13 = (f32[72,256]{1,0:T(8,128)S(1)}, f32[72,256]{1,0:T(8,128)S(1)}, u32[]{:S(2)}, u32[]{:S(2)}) collective-permute-start(f32[72,256]{1,0:T(8,128)S(1)} %fusion.1), channel_id=1, source_target_pairs={{0,224},{1,225},{2,226},{3,227},{4,228},{5,229},{6,230},{7,231},{8... | collective-permute-start | bytes 221192 | tf_op jit(solution)/shard_map/ppermute | solution.py:312
  53.4 0.1 broadcast_select_fusion.1
  53.5 1.5 %collective-permute-start.10 = (f32[128,256]{1,0:T(8,128)S(1)}, f32[128,256]{1,0:T(8,128)S(1)}, u32[]{:S(2)}, u32[]{:S(2)}) collective-permute-start(f32[128,256]{1,0:T(8,128)S(1)} %dynamic-slice_bitcast_fusion), channel_id=1, source_target_pairs={{0,8},{1,9},{2,10},{3,11},{4,12},{5,13},{6,14},{7,15},{8,0},{9,1},... | collective-permute-start | bytes 393224 | tf_op jit(solution)/shard_map/ppermute | solution.py:312
  55.0 2.7 %collective-permute-start.8 = (f32[128,256]{1,0:T(8,128)S(1)}, f32[128,256]{1,0:T(8,128)S(1)}, u32[]{:S(2)}, u32[]{:S(2)}) collective-permute-start(f32[128,256]{1,0:T(8,128)S(1)} %get-tuple-element.56), channel_id=1, source_target_pairs={{0,10},{1,11},{2,8},{3,9},{4,14},{5,15},{6,12},{7,13},{8,2},{9,3},... | collective-permute-start | bytes 393224 | tf_op jit(solution)/shard_map/ppermute | solution.py:312
  57.7 1.6 %collective-permute-start.9 = (f32[128,256]{1,0:T(8,128)S(1)}, f32[128,256]{1,0:T(8,128)S(1)}, u32[]{:S(2)}, u32[]{:S(2)}) collective-permute-start(f32[128,256]{1,0:T(8,128)S(1)} %get-tuple-element.55), channel_id=1, source_target_pairs={{0,2},{1,3},{2,0},{3,1},{4,6},{5,7},{6,4},{7,5},{8,10},{9,11},{10,... | collective-permute-start | bytes 393224 | tf_op jit(solution)/shard_map/ppermute | solution.py:312
  59.3 0.0 collective-permute-done.13
  59.4 1.7 %collective-permute-start.14 = (f32[72,256]{1,0:T(8,128)S(1)}, f32[72,256]{1,0:T(8,128)S(1)}, u32[]{:S(2)}, u32[]{:S(2)}) collective-permute-start(f32[72,256]{1,0:T(8,128)S(1)} %add.133), channel_id=1, source_target_pairs={{0,64},{1,65},{2,66},{3,67},{4,68},{5,69},{6,70},{7,71},{8,72},{9,... | collective-permute-start | bytes 221192 | tf_op jit(solution)/shard_map/ppermute | solution.py:312
  61.1 2.0 %collective-permute-done.14 = f32[72,256]{1,0:T(8,128)S(1)} collective-permute-done((f32[72,256]{1,0:T(8,128)S(1)}, f32[72,256]{1,0:T(8,128)S(1)}, u32[]{:S(2)}, u32[]{:S(2)}) %collective-permute-start.14) | collective-permute-done | bytes 73760 | tf_op jit(solution)/shard_map/ppermute | solution.py:312
  63.1 2.0 %collective-permute-start.15 = (f32[72,256]{1,0:T(8,128)S(1)}, f32[72,256]{1,0:T(8,128)S(1)}, u32[]{:S(2)}, u32[]{:S(2)}) collective-permute-start(f32[72,256]{1,0:T(8,128)S(1)} %add.134), channel_id=1, source_target_pairs={{0,32},{1,33},{2,34},{3,35},{4,36},{5,37},{6,38},{7,39},{8,40},{9,... | collective-permute-start | bytes 221192 | tf_op jit(solution)/shard_map/ppermute | solution.py:312
  65.1 0.0 collective-permute-done.10
  65.1 0.0 collective-permute-done.8
  65.1 0.0 collective-permute-done.9
  65.2 1.9 %collective-permute-start.11 = (f32[128,256]{1,0:T(8,128)S(1)}, f32[128,256]{1,0:T(8,128)S(1)}, u32[]{:S(2)}, u32[]{:S(2)}) collective-permute-start(f32[128,256]{1,0:T(8,128)S(1)} %fusion), channel_id=1, source_target_pairs={{0,32},{1,33},{2,34},{3,35},{4,36},{5,37},{6,38},{7,39},{8,40},{9,... | collective-permute-start | bytes 393224 | tf_op jit(solution)/shard_map/ppermute | solution.py:312
  67.1 2.6 %collective-permute-done.15 = f32[72,256]{1,0:T(8,128)S(1)} collective-permute-done((f32[72,256]{1,0:T(8,128)S(1)}, f32[72,256]{1,0:T(8,128)S(1)}, u32[]{:S(2)}, u32[]{:S(2)}) %collective-permute-start.15) | collective-permute-done | bytes 73760 | tf_op jit(solution)/shard_map/ppermute | solution.py:312
  69.7 6.8 %collective-permute-start.16 = (f32[72,256]{1,0:T(8,128)S(1)}, f32[72,256]{1,0:T(8,128)S(1)}, u32[]{:S(2)}, u32[]{:S(2)}) collective-permute-start(f32[72,256]{1,0:T(8,128)S(1)} %add.135), channel_id=1, source_target_pairs={{0,16},{1,17},{2,18},{3,19},{4,20},{5,21},{6,22},{7,23},{8,24},{9,... | collective-permute-start | bytes 221192 | tf_op jit(solution)/shard_map/ppermute | solution.py:312
  76.6 0.0 collective-permute-done.11
  76.6 0.9 collective-permute-done.16
  77.5 0.1 collective-permute-start.17
  77.6 5.3 %factorize_first.1 = (f32[256,256]{1,0:T(8,128)S(1)}, f32[256,64]{1,0:T(8,128)S(1)}, f32[8,256]{1,0:T(8,128)S(1)}) custom-call(f32[72,256]{1,0:T(8,128)S(1)} %get-tuple-element.35.corner_ref, f32[72,256]{1,0:T(8,128)S(1)} %get-tuple-element.36.mixed_ref), custom_call_target="tpu_custom_call" | custom-call | flops 6442450944 | bytes 1048576 | tf_op jit(solution)/shard_map/factorize_first/pallas_call | solution.py:266
  83.0 0.0 collective-permute-done.17
  83.0 0.0 copy-start
  83.0 0.3 collective-permute-start.18
  83.3 5.0 %factorize_second.1 = (f32[256,256]{1,0:T(8,128)}, f32[256,256]{1,0:T(8,128)S(1)}) custom-call(f32[256,256]{1,0:T(8,128)S(1)} %get-tuple-element.41.state_ref, f32[256,64]{1,0:T(8,128)S(1)} %get-tuple-element.42.upper_ref, f32[8,256]{1,0:T(8,128)S(1)} %get-tuple-element.43.scales_ref), custom_call_target="tpu_custom_call" | custom-call | flops 6442450944 | bytes 1048576 | tf_op jit(solution)/shard_map/factorize_second/pallas_call | solution.py:281
  88.3 0.0 collective-permute-done.18
  88.4 5.6 %collective-permute-start.19 = (f32[128,256]{1,0:T(8,128)S(1)}, f32[128,256]{1,0:T(8,128)S(1)}, u32[]{:S(2)}, u32[]{:S(2)}) collective-permute-start(f32[128,256]{1,0:T(8,128)S(1)} %add.137), channel_id=1, source_target_pairs={{0,16},{1,17},{2,18},{3,19},{4,20},{5,21},{6,22},{7,23},{8,24},{9,... | collective-permute-start | bytes 393224 | tf_op jit(solution)/shard_map/ppermute | solution.py:312
  94.0 0.0 copy-done
  94.0 1.8 %basis.1 = bf16[1024,256]{1,0:T(8,128)(2,1)} custom-call(f32[1024,256]{1,0:T(8,128)S(1)} %copy-done, f32[256,256]{1,0:T(8,128)S(1)} %get-tuple-element.46.inverse_ref), custom_call_target="tpu_custom_call" | custom-call | flops 2147483648 | bytes 1048576 | tf_op jit(solution)/shard_map/basis/pallas_call | solution.py:296
  95.8 0.0 collective-permute-done.19
  95.9 0.8 convolution_multiply_fusion
  (17 shorter events, 0.4 us)
Async XLA Ops:
  16.8 12.8 %copy-start.1 = (f32[2,4,128,256]{3,2,1,0:T(8,128)S(1)}, f32[2,4,128,256]{3,2,1,0:T(8,128)}, u32[]{:S(2)}) copy-start(f32[2,4,128,256]{3,2,1,0:T(8,128)} %get-tuple-element.27) | copy-start | bytes 3145732
  16.8 7.3 %collective-permute-start.2 = (f32[2,4,128,256]{3,2,1,0:T(8,128)}, f32[2,4,128,256]{3,2,1,0:T(8,128)S(1)}, u32[]{:S(2)}, u32[]{:S(2)}) collective-permute-start(f32[2,4,128,256]{3,2,1,0:T(8,128)} %get-tuple-element.33), channel_id=1, source_target_pairs={{0,16},{1,17},{2,18},{3,19},{4,20},{5,21},{6,22},{7,23},{8,24},{9,... | collective-permute-start | bytes 3145736 | tf_op jit(solution)/shard_map/ppermute | solution.py:312
  20.2 2.6 %collective-permute-start = (f32[72,256]{1,0:T(8,128)}, f32[72,256]{1,0:T(8,128)S(1)}, u32[]{:S(2)}, u32[]{:S(2)}) collective-permute-start(f32[72,256]{1,0:T(8,128)} %get-tuple-element.30), channel_id=1, source_target_pairs={{0,16},{1,17},{2,18},{3,19},{4,20},{5,21},{6,22},{7,23},{8,24},{9,... | collective-permute-start | bytes 221192 | tf_op jit(solution)/shard_map/ppermute | solution.py:312
  23.7 5.9 %collective-permute-start.1 = (f32[2,4,128,256]{3,2,1,0:T(8,128)}, f32[2,4,128,256]{3,2,1,0:T(8,128)S(1)}, u32[]{:S(2)}, u32[]{:S(2)}) collective-permute-start(f32[2,4,128,256]{3,2,1,0:T(8,128)} %get-tuple-element.31), channel_id=1, source_target_pairs={{0,16},{1,17},{2,18},{3,19},{4,20},{5,21},{6,22},{7,23},{8,24},{9,... | collective-permute-start | bytes 3145736 | tf_op jit(solution)/shard_map/ppermute | solution.py:312
  25.7 10.5 %collective-permute-start.3 = (f32[584,256]{1,0:T(8,128)S(1)}, f32[584,256]{1,0:T(8,128)}, u32[]{:S(2)}, u32[]{:S(2)}) collective-permute-start(f32[584,256]{1,0:T(8,128)S(1)} %get-tuple-element.62), channel_id=1, source_target_pairs={{0,3},{1,2},{2,1},{3,0},{4,7},{5,6},{6,5},{7,4},{8,11},{9,10},{10,... | collective-permute-start | bytes 1794056 | tf_op jit(solution)/shard_map/ppermute | solution.py:312
  26.8 10.6 %collective-permute-start.4 = (f32[584,256]{1,0:T(8,128)S(1)}, f32[584,256]{1,0:T(8,128)}, u32[]{:S(2)}, u32[]{:S(2)}) collective-permute-start(f32[584,256]{1,0:T(8,128)S(1)} %get-tuple-element.61), channel_id=1, source_target_pairs={{0,1},{1,0},{2,3},{3,2},{4,5},{5,4},{6,7},{7,6},{8,9},{9,8},{10,11... | collective-permute-start | bytes 1794056 | tf_op jit(solution)/shard_map/ppermute | solution.py:312
  26.8 11.8 %collective-permute-start.5 = (f32[72,256]{1,0:T(8,128)S(1)}, f32[72,256]{1,0:T(8,128)S(1)}, u32[]{:S(2)}, u32[]{:S(2)}) collective-permute-start(f32[72,256]{1,0:T(8,128)S(1)} %add.112), channel_id=1, source_target_pairs={{0,2},{1,3},{2,0},{3,1},{4,6},{5,7},{6,4},{7,5},{8,10},{9,11},{10,... | collective-permute-start | bytes 221192 | tf_op jit(solution)/shard_map/ppermute | solution.py:312
  39.6 9.5 %collective-permute-start.6 = (f32[328,256]{1,0:T(8,128)S(1)}, f32[328,256]{1,0:T(8,128)S(1)}, u32[]{:S(2)}, u32[]{:S(2)}) collective-permute-start(f32[328,256]{1,0:T(8,128)S(1)} %get-tuple-element.60), channel_id=1, source_target_pairs={{0,12},{1,13},{2,14},{3,15},{4,8},{5,9},{6,10},{7,11},{8,4},{9,5},... | collective-permute-start | bytes 1007624 | tf_op jit(solution)/shard_map/ppermute | solution.py:312
  40.9 8.1 %collective-permute-start.7 = (f32[328,256]{1,0:T(8,128)S(1)}, f32[328,256]{1,0:T(8,128)S(1)}, u32[]{:S(2)}, u32[]{:S(2)}) collective-permute-start(f32[328,256]{1,0:T(8,128)S(1)} %get-tuple-element.59), channel_id=1, source_target_pairs={{0,4},{1,5},{2,6},{3,7},{4,0},{5,1},{6,2},{7,3},{8,12},{9,13},{10,... | collective-permute-start | bytes 1007624 | tf_op jit(solution)/shard_map/ppermute | solution.py:312
  40.9 8.1 %collective-permute-start.12 = (f32[72,256]{1,0:T(8,128)S(1)}, f32[72,256]{1,0:T(8,128)S(1)}, u32[]{:S(2)}, u32[]{:S(2)}) collective-permute-start(f32[72,256]{1,0:T(8,128)S(1)} %fusion.2), channel_id=1, source_target_pairs={{0,8},{1,9},{2,10},{3,11},{4,12},{5,13},{6,14},{7,15},{8,0},{9,1},... | collective-permute-start | bytes 221192 | tf_op jit(solution)/shard_map/ppermute | solution.py:312
  49.1 10.3 %collective-permute-start.13 = (f32[72,256]{1,0:T(8,128)S(1)}, f32[72,256]{1,0:T(8,128)S(1)}, u32[]{:S(2)}, u32[]{:S(2)}) collective-permute-start(f32[72,256]{1,0:T(8,128)S(1)} %fusion.1), channel_id=1, source_target_pairs={{0,224},{1,225},{2,226},{3,227},{4,228},{5,229},{6,230},{7,231},{8... | collective-permute-start | bytes 221192 | tf_op jit(solution)/shard_map/ppermute | solution.py:312
  53.5 11.6 %collective-permute-start.10 = (f32[128,256]{1,0:T(8,128)S(1)}, f32[128,256]{1,0:T(8,128)S(1)}, u32[]{:S(2)}, u32[]{:S(2)}) collective-permute-start(f32[128,256]{1,0:T(8,128)S(1)} %dynamic-slice_bitcast_fusion), channel_id=1, source_target_pairs={{0,8},{1,9},{2,10},{3,11},{4,12},{5,13},{6,14},{7,15},{8,0},{9,1},... | collective-permute-start | bytes 393224 | tf_op jit(solution)/shard_map/ppermute | solution.py:312
  55.0 10.1 %collective-permute-start.8 = (f32[128,256]{1,0:T(8,128)S(1)}, f32[128,256]{1,0:T(8,128)S(1)}, u32[]{:S(2)}, u32[]{:S(2)}) collective-permute-start(f32[128,256]{1,0:T(8,128)S(1)} %get-tuple-element.56), channel_id=1, source_target_pairs={{0,10},{1,11},{2,8},{3,9},{4,14},{5,15},{6,12},{7,13},{8,2},{9,3},... | collective-permute-start | bytes 393224 | tf_op jit(solution)/shard_map/ppermute | solution.py:312
  57.7 7.4 %collective-permute-start.9 = (f32[128,256]{1,0:T(8,128)S(1)}, f32[128,256]{1,0:T(8,128)S(1)}, u32[]{:S(2)}, u32[]{:S(2)}) collective-permute-start(f32[128,256]{1,0:T(8,128)S(1)} %get-tuple-element.55), channel_id=1, source_target_pairs={{0,2},{1,3},{2,0},{3,1},{4,6},{5,7},{6,4},{7,5},{8,10},{9,11},{10,... | collective-permute-start | bytes 393224 | tf_op jit(solution)/shard_map/ppermute | solution.py:312
  59.4 3.8 %collective-permute-start.14 = (f32[72,256]{1,0:T(8,128)S(1)}, f32[72,256]{1,0:T(8,128)S(1)}, u32[]{:S(2)}, u32[]{:S(2)}) collective-permute-start(f32[72,256]{1,0:T(8,128)S(1)} %add.133), channel_id=1, source_target_pairs={{0,64},{1,65},{2,66},{3,67},{4,68},{5,69},{6,70},{7,71},{8,72},{9,... | collective-permute-start | bytes 221192 | tf_op jit(solution)/shard_map/ppermute | solution.py:312
  63.1 6.6 %collective-permute-start.15 = (f32[72,256]{1,0:T(8,128)S(1)}, f32[72,256]{1,0:T(8,128)S(1)}, u32[]{:S(2)}, u32[]{:S(2)}) collective-permute-start(f32[72,256]{1,0:T(8,128)S(1)} %add.134), channel_id=1, source_target_pairs={{0,32},{1,33},{2,34},{3,35},{4,36},{5,37},{6,38},{7,39},{8,40},{9,... | collective-permute-start | bytes 221192 | tf_op jit(solution)/shard_map/ppermute | solution.py:312
  65.2 11.4 %collective-permute-start.11 = (f32[128,256]{1,0:T(8,128)S(1)}, f32[128,256]{1,0:T(8,128)S(1)}, u32[]{:S(2)}, u32[]{:S(2)}) collective-permute-start(f32[128,256]{1,0:T(8,128)S(1)} %fusion), channel_id=1, source_target_pairs={{0,32},{1,33},{2,34},{3,35},{4,36},{5,37},{6,38},{7,39},{8,40},{9,... | collective-permute-start | bytes 393224 | tf_op jit(solution)/shard_map/ppermute | solution.py:312
  69.7 7.8 %collective-permute-start.16 = (f32[72,256]{1,0:T(8,128)S(1)}, f32[72,256]{1,0:T(8,128)S(1)}, u32[]{:S(2)}, u32[]{:S(2)}) collective-permute-start(f32[72,256]{1,0:T(8,128)S(1)} %add.135), channel_id=1, source_target_pairs={{0,16},{1,17},{2,18},{3,19},{4,20},{5,21},{6,22},{7,23},{8,24},{9,... | collective-permute-start | bytes 221192 | tf_op jit(solution)/shard_map/ppermute | solution.py:312
  77.5 5.5 %collective-permute-start.17 = (f32[128,256]{1,0:T(8,128)S(1)}, f32[128,256]{1,0:T(8,128)S(1)}, u32[]{:S(2)}, u32[]{:S(2)}) collective-permute-start(f32[128,256]{1,0:T(8,128)S(1)} %add.129), channel_id=1, source_target_pairs={{0,64},{1,65},{2,66},{3,67},{4,68},{5,69},{6,70},{7,71},{8,72},{9,... | collective-permute-start | bytes 393224 | tf_op jit(solution)/shard_map/ppermute | solution.py:312
  83.0 11.0 %copy-start = (f32[1024,256]{1,0:T(8,128)S(1)}, f32[1024,256]{1,0:T(8,128)}, u32[]{:S(2)}) copy-start(f32[1024,256]{1,0:T(8,128)} %get-tuple-element.26.sketched_ref) | copy-start | bytes 3145732
  83.0 5.3 %collective-permute-start.18 = (f32[128,256]{1,0:T(8,128)S(1)}, f32[128,256]{1,0:T(8,128)S(1)}, u32[]{:S(2)}, u32[]{:S(2)}) collective-permute-start(f32[128,256]{1,0:T(8,128)S(1)} %add.136), channel_id=1, source_target_pairs={{0,224},{1,225},{2,226},{3,227},{4,228},{5,229},{6,230},{7,231},{8... | collective-permute-start | bytes 393224 | tf_op jit(solution)/shard_map/ppermute | solution.py:312
  88.4 7.5 %collective-permute-start.19 = (f32[128,256]{1,0:T(8,128)S(1)}, f32[128,256]{1,0:T(8,128)S(1)}, u32[]{:S(2)}, u32[]{:S(2)}) collective-permute-start(f32[128,256]{1,0:T(8,128)S(1)} %add.137), channel_id=1, source_target_pairs={{0,16},{1,17},{2,18},{3,19},{4,20},{5,21},{6,22},{7,23},{8,24},{9,... | collective-permute-start | bytes 393224 | tf_op jit(solution)/shard_map/ppermute | solution.py:312

commit v2 on v1

--- a/solution.py
+++ b/solution.py
@@ -32,14 +32,21 @@
     return jnp.dot(left, right, preferred_element_type=F32)
 
 
+def position():
+    core, place = lax.axis_index("gx") % 2, lax.axis_index("gy")
+    x, y = place % SIDE, place // SIDE
+    return core, jnp.where(core == 0, x, y), jnp.where(core == 0, y, x)
+
+
 def front_kernel(
-    where_ref, rows_hbm, sketch_hbm, sketched_hbm, piece_ref, piece_away_ref, away_send, away_keep, send, keep,
-    rows, sketch, sketched, split, blocks, row_sems, sketch_sems, sketched_sem, away_sems, own_sems, *, scale,
+    rows_hbm, sketch_hbm, sketched_hbm, away_send, away_keep, send, keep,
+    rows, sketch, sketched, split, blocks, pieces, row_sems, sketch_sems, sketched_sem, away_sems, own_sems, piece_sems,
+    *, scale,
 ):
     depth = rows.shape[1] // CHUNKS
     rank = sketched.shape[1]
     half, width = blocks.shape[2:]
-    core = where_ref[0]
+    core, outer_place, inner_place = position()
     copies = []
     for c in range(CHUNKS):
         part = pl.ds(c * depth, depth)
@@ -75,11 +82,20 @@
     diagonal = jnp.sum(jnp.where(row == col, end, 0.0), axis=0, keepdims=True)
     corner, mixed = gram[:half, half:], jnp.where(row <= col, gram[:half, :half], end)
     upper = half // 2
-    for ref, first in ((piece_ref, core == 0), (piece_away_ref, core == 1)):
+    for at, first in ((0, core == 0), (1, core == 1)):
         value = jnp.where(first, corner, mixed)
-        ref[:upper, :half] = value[:upper]
-        ref[:upper, half:] = value[upper:]
-        ref[upper:, :] = jnp.broadcast_to(jnp.concatenate([diagonal, diagonal], axis=1), (8, rank))
+        pieces[at, :upper, :half] = value[:upper]
+        pieces[at, :upper, half:] = value[upper:]
+        pieces[at, upper:, :] = jnp.broadcast_to(jnp.concatenate([diagonal, diagonal], axis=1), (8, rank))
+    pieces[2] = jnp.zeros_like(pieces[2])
+    tail = pl.ds(SIDE * half, pieces.shape[1])
+    tails = []
+    for at, ref, side in (
+        (0, send, 0), (0, send, 1), (0, keep, 0), (2, keep, 1),
+        (1, away_send, 0), (1, away_send, 1), (1, away_keep, 0), (2, away_keep, 1),
+    ):
+        tails.append(pltpu.make_async_copy(pieces.at[at], ref.at[side, tail], piece_sems.at[len(tails)]))
+        tails[-1].start()
 
     outs = []
     for y in range(SIDE):
@@ -90,50 +106,53 @@
             blocks[0, slot] = both[:half]
             blocks[1, slot] = both[half:]
             for which, bit, refs, sems in (
-                (1 - core, where_ref[2], (away_send, away_keep), away_sems),
-                (core, where_ref[1], (send, keep), own_sems),
+                (1 - core, inner_place % 2, (away_send, away_keep), away_sems),
+                (core, outer_place % 2, (send, keep), own_sems),
             ):
                 outer, inner = jnp.where(which == 0, x, y), jnp.where(which == 0, y, x)
                 stays = outer % 2 == bit
                 for ref, wanted in zip(refs, (jnp.logical_not(stays), stays)):
-                    to = ref.at[outer // 2, inner]
+                    to = ref.at[outer // 2, pl.ds(pl.multiple_of(inner * half, half), half)]
                     copy = pltpu.make_async_copy(blocks.at[which, slot], to, sems.at[slot])
                     pl.when(wanted)(copy.start)
                     outs.append((wanted, copy))
     for wanted, copy in outs:
         pl.when(wanted)(copy.wait)
     sketched_copy.wait()
-
-
-def front(where, embeddings, sketch, scale):
+    for copy in tails:
+        copy.wait()
+
+
+def front(embeddings, sketch, scale):
     count, width = embeddings.shape
     rank = sketch.shape[1]
     half = rank // 2
     hbm = pl.BlockSpec(memory_space=pl.ANY)
-    vmem = pl.BlockSpec(memory_space=pltpu.VMEM)
-    piece = jax.ShapeDtypeStruct((half // 2 + 8, rank), F32)
-    term = jax.ShapeDtypeStruct((SIDE // 2, SIDE, half, width // SIDE**2), F32)
+    piece = half // 2 + 8
+    term = jax.ShapeDtypeStruct((SIDE // 2, SIDE * half + piece, rank), F32)
     return pl.pallas_call(
         functools.partial(front_kernel, scale=scale),
-        in_specs=[pl.BlockSpec(memory_space=pltpu.SMEM), hbm, hbm],
-        out_specs=[hbm, vmem, vmem, hbm, hbm, hbm, hbm],
-        out_shape=[jax.ShapeDtypeStruct((count, rank), F32), piece, piece, term, term, term, term],
+        in_specs=[hbm, hbm],
+        out_specs=[hbm] * 5,
+        out_shape=[jax.ShapeDtypeStruct((count, rank), F32), term, term, term, term],
         scratch_shapes=[
             pltpu.VMEM((count, width), BF16),
             pltpu.VMEM((width, rank), BF16),
             pltpu.VMEM((count, rank), F32),
             pltpu.VMEM((2 * rank, count), BF16),
             pltpu.VMEM((2, SIDE**2, half, width // SIDE**2), F32),
+            pltpu.VMEM((3, piece, rank), F32),
             pltpu.SemaphoreType.DMA((CHUNKS,)),
             pltpu.SemaphoreType.DMA((CHUNKS,)),
             pltpu.SemaphoreType.DMA,
             pltpu.SemaphoreType.DMA((SIDE**2,)),
             pltpu.SemaphoreType.DMA((SIDE**2,)),
+            pltpu.SemaphoreType.DMA((8,)),
         ],
         compiler_params=pltpu.CompilerParams(vmem_limit_bytes=LIMIT),
         cost_estimate=pl.CostEstimate(flops=6 * count * width * rank, bytes_accessed=2**24, transcendentals=0),
         name="front",
-    )(where, embeddings, sketch)
+    )(embeddings, sketch)
 
 
 def eliminate(pair, size):
@@ -317,7 +336,7 @@
 CORE = ((1, 0), (1, 0))
 
 
-X3, Y3, XY2 = (0, 3), (0, 12), (0, 10)
+X3, Y3 = (0, 3), (0, 12)
 
 
 def halves(value, bit, dim):
@@ -342,40 +361,29 @@
 def body(embeddings, sketch):
     total_rows = embeddings.shape[0] * lax.axis_size("gx") * lax.axis_size("gy")
     rank = sketch.shape[1]
-    core = lax.axis_index("gx") % 2
-    place = lax.axis_index("gy")
-    x, y = place % SIDE, place // SIDE
-    outer, inner = jnp.where(core == 0, x, y), jnp.where(core == 0, y, x)
-    where = jnp.stack([core, outer % 2, inner % 2]).astype(jnp.int32)
-    sketched, piece, piece_away, *terms = front(where, embeddings, sketch, 1.0 / total_rows)
-    away_send, away_keep, send, keep = terms
-    half, width = keep.shape[2:]
-
-    piece = piece + trade(piece_away, CORE)
-    send = send + trade(away_send, CORE)
-    keep = keep + trade(after(away_keep, piece), CORE)
-    one, piece_1 = trade_both(send[0], piece, (X1, Y1))
-    three, piece_3 = trade_both(send[1], piece, (X3, Y3))
-    piece = (piece + piece_1) + (trade(piece, (X2, Y2)) + piece_3)
-    terms = [(k + got).reshape(2, 2, half, width) for k, got in zip(keep, (one, three))]
+    core, outer, inner = position()
+    sketched, away_send, away_keep, send, keep = front(embeddings, sketch, 1.0 / total_rows)
+    half = rank // 2
+    rows = SIDE * half
+
+    message = send + trade(away_send, CORE)
+    keep = keep + trade(after(away_keep, message), CORE)
+    one = keep[0] + trade(message[0], (X1, Y1))
+    three = keep[1] + trade(message[1], (X3, Y3))
+    piece = one[rows:] + (trade(message[0, rows:], (X2, Y2)) + three[rows:])
+    terms = [part[:rows].reshape(2, 2, half, -1) for part in (one, three)]
     parts = [halves(term, inner % 2, 1) for term in terms]
     one, piece_1 = trade_both(parts[0][1], piece, (Y1, X1))
     three, piece_3 = trade_both(parts[1][1], piece, (Y3, X3))
     piece = (piece + piece_1) + (trade(piece, (Y2, X2)) + piece_3)
     low, high = (part[0] + got for part, got in zip(parts, (one, three)))
-    outer, inner = outer // 2, inner // 2
-
-    def quarter(across, along):
-        pair = jnp.where((outer ^ across) == 1, high, low)
-        return lax.dynamic_index_in_dim(pair, inner ^ along, 0, keepdims=False)
-
-    one = trade(quarter(1, 1), (XY2, XY2))
-    two = trade(quarter(1, 0), (X2, Y2))
-    three = trade(quarter(0, 1), (Y2, X2))
+    upper = outer // 2 == 1
+    term = jnp.where(upper, high, low) + trade(jnp.where(upper, low, high), (X2, Y2))
     piece = piece + trade(piece, (Z7, Z7))
-    term = (quarter(0, 0) + one) + (two + three)
+    keep, send = halves(term, inner // 2, 0)
+    term = keep + trade(send, (Y2, X2))
     piece = piece + trade(piece, (Z2, Z1))
-    piece = piece + trade(piece, (Z1, Z2))
+    piece = piece + trade(after(piece, term), (Z1, Z2))
 
     other = trade(piece, CORE)
     corner, mixed = jnp.where(core == 0, piece, other), jnp.where(core == 0, other, piece)
@@ -389,7 +397,7 @@
     term = term + trade(term, (Z7, Z7))
     term, factor, inverse = lax.optimization_barrier((term, factor, inverse))
     basis = basis_of(sketched, inverse)
-    summed = order(core, term, trade(term, CORE)).reshape(rank, width)
+    summed = order(core, term, trade(term, CORE)).reshape(rank, -1)
 
     row_count = rank // lax.axis_size("gx")
     mine = lax.dynamic_slice_in_dim(inverse, lax.axis_index("gx") * row_count, row_count, 0)

time: 97 us -> 93.3 us (0.962)
  starting transfers between devices: 40.5 us -> 34.3 us
  waiting for transfers between devices: 19.8 us -> 24.9 us
  Pallas kernels: 27.7 us -> 26.5 us
  local copies, waits for them, and re-layouts: 2.46 us -> 1.33 us
    ppermute x20 -> x18, starting transfers between devices: 40.5 us -> 34.3 us  [trade(): return lax.ppermute(value, ('gx', 'gy'), pairs)]
    ppermute x20 -> x18, waiting for transfers between devices: 19.8 us -> 24.9 us  [trade(): return lax.ppermute(value, ('gx', 'gy'), pairs)]
    slice x4 -> x2, local copies, waits for them, and re-layouts: 2.19 us -> 0.04 us  [trade_both(): return (got[:flat.shape[0]].reshape(value.shape), got[flat.shape[0]:])]
    pallas_call x1, Pallas kernels: 15.5 us -> 14.3 us  [front(): pl.pallas_call(functools.partial(front_kernel, scale=scale), in_specs=[hb...]
    squeeze x2 -> x3, local copies, waits for them, and re-layouts: 0.04 us -> 1.17 us  [the longest x1 1.14 us: body(): one = keep[0] + trade(message[0], (X1, Y1))]
    add x8 -> x7, other arithmetic: 3.53 us -> 4.24 us  [the longest x1 1.43 us: body(): message = send + trade(away_send, CORE)]
  transfers between devices with their start and end apart: 20 -> 18, of which waited for: 6 -> 8; matrix products, arithmetic and copies ran while one was open for 5% -> 5% of each run, Pallas kernels for 13% -> 13%
where the time goes in v2:
time: 93.3 us; the launch traced here: 93.1 us
  starting transfers between devices  34.3 us (37%)
  Pallas kernels  26.5 us (28%)
  waiting for transfers between devices  24.9 us (27%)
  other arithmetic  4.49 us (5%)
  local copies, waits for them, and re-layouts  1.33 us (1%)
    ppermute x18, starting transfers between devices, trade(): return lax.ppermute(value, ('gx', 'gy'), pairs)  34.3 us
    ppermute x18, waiting for transfers between devices, trade(): return lax.ppermute(value, ('gx', 'gy'), pairs)  24.9 us
    pallas_call x1, Pallas kernels, front(): pl.pallas_call(functools.partial(front_kernel, scale=scale), in_specs=[hb...  14.3 us
    pallas_call x1, Pallas kernels, factorize_first(): pl.pallas_call(functools.partial(first_kernel, block=block), out_shape=[j...  5.35 us
    pallas_call x1, Pallas kernels, factorize_second(): pl.pallas_call(functools.partial(second_kernel, block=block), out_shape=[...  4.97 us
  transfers between devices with their start and end apart: 18, of which 8 were waited for; matrix products, arithmetic and copies ran while one was open for 5% of the time, Pallas kernels for 13%

profile of v2, /device:TPU:1, one launch (start us, length us, event | category | flops | bytes accessed | tf_op | source)
XLA Modules:
  0.0 93.1 jit_solution(4577916093037969412)
XLA Ops:
  0.6 14.3 %front.1 = (f32[1024,256]{1,0:T(8,128)}, f32[2,584,256]{2,1,0:T(8,128)}, f32[2,584,256]{2,1,0:T(8,128)}, f32[2,584,256]{2,1,0:T(8,128)}, f32[2,584,256]{2,1,0:T(8,128)}) custom-call(bf16[1024,4096]{1,0:T(8,128)(2,1)} %rows_hbm.1, bf16[4096,256]{1,0:T(8,128)(2,1)} %sketch_hbm.1), custom_call_target="tpu_custom_call" | custom-call | flops 6442450944 | bytes 16777216 | tf_op jit(solution)/shard_map/front/pallas_call | solution.py:133
  15.0 3.3 %collective-permute-start = (f32[2,584,256]{2,1,0:T(8,128)}, f32[2,584,256]{2,1,0:T(8,128)S(1)}, u32[]{:S(2)}, u32[]{:S(2)}) collective-permute-start(f32[2,584,256]{2,1,0:T(8,128)} %get-tuple-element.29), channel_id=1, source_target_pairs={{0,16},{1,17},{2,18},{3,19},{4,20},{5,21},{6,22},{7,23},{8,24},{9,... | collective-permute-start | bytes 3588104 | tf_op jit(solution)/shard_map/ppermute | solution.py:331
  18.3 2.7 %collective-permute-done = f32[2,584,256]{2,1,0:T(8,128)S(1)} collective-permute-done((f32[2,584,256]{2,1,0:T(8,128)}, f32[2,584,256]{2,1,0:T(8,128)S(1)}, u32[]{:S(2)}, u32[]{:S(2)}) %collective-permute-start) | collective-permute-done | bytes 1196064 | tf_op jit(solution)/shard_map/ppermute | solution.py:331
  21.0 1.4 %add.94 = f32[2,584,256]{2,1,0:T(8,128)S(1)} add(f32[2,584,256]{2,1,0:T(8,128)} %get-tuple-element.28, f32[2,584,256]{2,1,0:T(8,128)S(1)} %collective-permute-done) | non-fusion elementwise | flops 299008 | bytes 3588096 | tf_op jit(solution)/shard_map/add | solution.py:369
  22.4 0.0 copy-start.1
  22.5 0.5 collective-permute-start.1
  22.9 1.1 %slice_bitcast_fusion = (f32[584,256]{1,0:T(8,128)}, f32[584,256]{1,0:T(8,128)}) fusion(f32[2,584,256]{2,1,0:T(8,128)S(1)} %add.94), kind=kLoop, calls=%fused_computation.1 | loop fusion | bytes 2392064 | tf_op jit(solution)/shard_map/squeeze | solution.py:371
  24.1 0.0 collective-permute-start.3
  24.1 1.5 %collective-permute-start.2 = (f32[584,256]{1,0:T(8,128)}, f32[584,256]{1,0:T(8,128)}, u32[]{:S(2)}, u32[]{:S(2)}) collective-permute-start(f32[584,256]{1,0:T(8,128)} %get-tuple-element.50), channel_id=1, source_target_pairs={{0,3},{1,2},{2,1},{3,0},{4,7},{5,6},{6,5},{7,4},{8,11},{9,10},{10,... | collective-permute-start | bytes 1794056 | tf_op jit(solution)/shard_map/ppermute | solution.py:331
  25.5 1.8 %collective-permute-start.4 = (f32[72,256]{1,0:T(8,128)S(1)}, f32[72,256]{1,0:T(8,128)S(1)}, u32[]{:S(2)}, u32[]{:S(2)}) collective-permute-start(f32[72,256]{1,0:T(8,128)S(1)} %slice_bitcast_fusion.4), channel_id=1, source_target_pairs={{0,2},{1,3},{2,0},{3,1},{4,6},{5,7},{6,4},{7,5},{8,10},{9,11},{10,... | collective-permute-start | bytes 221192 | tf_op jit(solution)/shard_map/ppermute | solution.py:331
  27.3 0.0 collective-permute-done.1
  27.3 0.0 copy-done.1
  27.3 1.4 %add.95 = f32[2,584,256]{2,1,0:T(8,128)S(1)} add(f32[2,584,256]{2,1,0:T(8,128)S(1)} %copy-done.1, f32[2,584,256]{2,1,0:T(8,128)} %collective-permute-done.1) | non-fusion elementwise | flops 299008 | bytes 3588096 | tf_op jit(solution)/shard_map/add | solution.py:370
  28.8 4.7 %collective-permute-done.3 = f32[584,256]{1,0:T(8,128)S(1)} collective-permute-done((f32[584,256]{1,0:T(8,128)}, f32[584,256]{1,0:T(8,128)S(1)}, u32[]{:S(2)}, u32[]{:S(2)}) %collective-permute-start.3) | collective-permute-done | bytes 598048 | tf_op jit(solution)/shard_map/ppermute | solution.py:331
  33.5 2.0 %collective-permute-done.2 = f32[584,256]{1,0:T(8,128)} collective-permute-done((f32[584,256]{1,0:T(8,128)}, f32[584,256]{1,0:T(8,128)}, u32[]{:S(2)}, u32[]{:S(2)}) %collective-permute-start.2) | collective-permute-done | bytes 598048 | tf_op jit(solution)/shard_map/ppermute | solution.py:331
  35.5 1.2 %fusion = (f32[584,256]{1,0:T(8,128)S(1)}, f32[584,256]{1,0:T(8,128)S(1)}) fusion(f32[584,256]{1,0:T(8,128)S(1)} %collective-permute-done.3, f32[2,584,256]{2,1,0:T(8,128)S(1)} %add.95, f32[584,256]{1,0:T(8,128)} %collective-permute-done.2), kind=kLoop, calls=%fused_computation.3 | loop fusion | flops 299008 | bytes 3588096 | tf_op jit(solution)/shard_map/add | solution.py:371
  36.9 0.0 collective-permute-done.4
  36.9 1.4 %collective-permute-start.5 = (f32[328,256]{1,0:T(8,128)S(1)}, f32[328,256]{1,0:T(8,128)S(1)}, u32[]{:S(2)}, u32[]{:S(2)}) collective-permute-start(f32[328,256]{1,0:T(8,128)S(1)} %get-tuple-element.54), channel_id=1, source_target_pairs={{0,12},{1,13},{2,14},{3,15},{4,8},{5,9},{6,10},{7,11},{8,4},{9,5},... | collective-permute-start | bytes 1007624 | tf_op jit(solution)/shard_map/ppermute | solution.py:331
  38.3 0.0 collective-permute-start.6
  38.3 2.6 %collective-permute-start.10 = (f32[72,256]{1,0:T(8,128)S(1)}, f32[72,256]{1,0:T(8,128)S(1)}, u32[]{:S(2)}, u32[]{:S(2)}) collective-permute-start(f32[72,256]{1,0:T(8,128)S(1)} %fusion.3), channel_id=1, source_target_pairs={{0,8},{1,9},{2,10},{3,11},{4,12},{5,13},{6,14},{7,15},{8,0},{9,1},... | collective-permute-start | bytes 221192 | tf_op jit(solution)/shard_map/ppermute | solution.py:331
  40.9 3.7 %collective-permute-done.5 = f32[328,256]{1,0:T(8,128)S(1)} collective-permute-done((f32[328,256]{1,0:T(8,128)S(1)}, f32[328,256]{1,0:T(8,128)S(1)}, u32[]{:S(2)}, u32[]{:S(2)}) %collective-permute-start.5) | collective-permute-done | bytes 335904 | tf_op jit(solution)/shard_map/ppermute | solution.py:331
  44.6 0.0 collective-permute-done.6
  44.6 0.1 broadcast_select_fusion
  44.7 2.3 %collective-permute-start.7 = (f32[2,128,256]{2,1,0:T(8,128)S(1)}, f32[2,128,256]{2,1,0:T(8,128)S(1)}, u32[]{:S(2)}, u32[]{:S(2)}) collective-permute-start(f32[2,128,256]{2,1,0:T(8,128)S(1)} %broadcast_select_fusion), channel_id=1, source_target_pairs={{0,2},{1,3},{2,0},{3,1},{4,6},{5,7},{6,4},{7,5},{8,10},{9,11},{10,... | collective-permute-start | bytes 786440 | tf_op jit(solution)/shard_map/ppermute | solution.py:331
  47.0 0.0 collective-permute-done.10
  47.0 5.7 %collective-permute-start.11 = (f32[72,256]{1,0:T(8,128)S(1)}, f32[72,256]{1,0:T(8,128)S(1)}, u32[]{:S(2)}, u32[]{:S(2)}) collective-permute-start(f32[72,256]{1,0:T(8,128)S(1)} %fusion.2), channel_id=1, source_target_pairs={{0,224},{1,225},{2,226},{3,227},{4,228},{5,229},{6,230},{7,231},{8... | collective-permute-start | bytes 221192 | tf_op jit(solution)/shard_map/ppermute | solution.py:331
  52.7 0.0 collective-permute-done.7
  52.7 0.1 select_add_fusion
  52.8 0.5 collective-permute-start.8
  53.3 2.2 %collective-permute-done.11 = f32[72,256]{1,0:T(8,128)S(1)} collective-permute-done((f32[72,256]{1,0:T(8,128)S(1)}, f32[72,256]{1,0:T(8,128)S(1)}, u32[]{:S(2)}, u32[]{:S(2)}) %collective-permute-start.11) | collective-permute-done | bytes 73760 | tf_op jit(solution)/shard_map/ppermute | solution.py:331
  55.5 0.7 collective-permute-start.12
  56.3 3.1 %collective-permute-done.12 = f32[72,256]{1,0:T(8,128)S(1)} collective-permute-done((f32[72,256]{1,0:T(8,128)S(1)}, f32[72,256]{1,0:T(8,128)S(1)}, u32[]{:S(2)}, u32[]{:S(2)}) %collective-permute-start.12) | collective-permute-done | bytes 73760 | tf_op jit(solution)/shard_map/ppermute | solution.py:331
  59.3 0.0 collective-permute-done.8
  59.4 1.1 %collective-permute-start.13 = (f32[72,256]{1,0:T(8,128)S(1)}, f32[72,256]{1,0:T(8,128)S(1)}, u32[]{:S(2)}, u32[]{:S(2)}) collective-permute-start(f32[72,256]{1,0:T(8,128)S(1)} %add.114), channel_id=1, source_target_pairs={{0,32},{1,33},{2,34},{3,35},{4,36},{5,37},{6,38},{7,39},{8,40},{9,... | collective-permute-start | bytes 221192 | tf_op jit(solution)/shard_map/ppermute | solution.py:331
  60.5 1.3 %collective-permute-start.9 = (f32[128,256]{1,0:T(8,128)S(1)}, f32[128,256]{1,0:T(8,128)S(1)}, u32[]{:S(2)}, u32[]{:S(2)}) collective-permute-start(f32[128,256]{1,0:T(8,128)S(1)} %bitcast_add_fusion.2), channel_id=1, source_target_pairs={{0,32},{1,33},{2,34},{3,35},{4,36},{5,37},{6,38},{7,39},{8,40},{9,... | collective-permute-start | bytes 393224 | tf_op jit(solution)/shard_map/ppermute | solution.py:331
  61.8 5.6 %collective-permute-done.13 = f32[72,256]{1,0:T(8,128)S(1)} collective-permute-done((f32[72,256]{1,0:T(8,128)S(1)}, f32[72,256]{1,0:T(8,128)S(1)}, u32[]{:S(2)}, u32[]{:S(2)}) %collective-permute-start.13) | collective-permute-done | bytes 73760 | tf_op jit(solution)/shard_map/ppermute | solution.py:331
  67.4 5.0 %collective-permute-start.14 = (f32[72,256]{1,0:T(8,128)S(1)}, f32[72,256]{1,0:T(8,128)S(1)}, u32[]{:S(2)}, u32[]{:S(2)}) collective-permute-start(f32[72,256]{1,0:T(8,128)S(1)} %add.115), channel_id=1, source_target_pairs={{0,16},{1,17},{2,18},{3,19},{4,20},{5,21},{6,22},{7,23},{8,24},{9,... | collective-permute-start | bytes 221192 | tf_op jit(solution)/shard_map/ppermute | solution.py:331
  72.4 0.0 collective-permute-done.9
  72.4 0.9 collective-permute-done.14
  73.3 0.1 collective-permute-start.15
  73.4 5.3 %factorize_first.1 = (f32[256,256]{1,0:T(8,128)S(1)}, f32[256,64]{1,0:T(8,128)S(1)}, f32[8,256]{1,0:T(8,128)S(1)}) custom-call(f32[72,256]{1,0:T(8,128)S(1)} %get-tuple-element.33.corner_ref, f32[72,256]{1,0:T(8,128)S(1)} %get-tuple-element.34.mixed_ref), custom_call_target="tpu_custom_call" | custom-call | flops 6442450944 | bytes 1048576 | tf_op jit(solution)/shard_map/factorize_first/pallas_call | solution.py:285
  78.8 0.0 collective-permute-done.15
  78.8 0.0 copy-start
  78.8 3.9 %collective-permute-start.16 = (f32[128,256]{1,0:T(8,128)S(1)}, f32[128,256]{1,0:T(8,128)S(1)}, u32[]{:S(2)}, u32[]{:S(2)}) collective-permute-start(f32[128,256]{1,0:T(8,128)S(1)} %add.116), channel_id=1, source_target_pairs={{0,224},{1,225},{2,226},{3,227},{4,228},{5,229},{6,230},{7,231},{8... | collective-permute-start | bytes 393224 | tf_op jit(solution)/shard_map/ppermute | solution.py:331
  82.7 5.0 %factorize_second.1 = (f32[256,256]{1,0:T(8,128)}, f32[256,256]{1,0:T(8,128)S(1)}) custom-call(f32[256,256]{1,0:T(8,128)S(1)} %get-tuple-element.39.state_ref, f32[256,64]{1,0:T(8,128)S(1)} %get-tuple-element.40.upper_ref, f32[8,256]{1,0:T(8,128)S(1)} %get-tuple-element.41.scales_ref), custom_call_target="tpu_custom_call" | custom-call | flops 6442450944 | bytes 1048576 | tf_op jit(solution)/shard_map/factorize_second/pallas_call | solution.py:300
  87.7 0.0 collective-permute-done.16
  87.7 2.7 %collective-permute-start.17 = (f32[128,256]{1,0:T(8,128)S(1)}, f32[128,256]{1,0:T(8,128)S(1)}, u32[]{:S(2)}, u32[]{:S(2)}) collective-permute-start(f32[128,256]{1,0:T(8,128)S(1)} %add.117), channel_id=1, source_target_pairs={{0,16},{1,17},{2,18},{3,19},{4,20},{5,21},{6,22},{7,23},{8,24},{9,... | collective-permute-start | bytes 393224 | tf_op jit(solution)/shard_map/ppermute | solution.py:331
  90.4 0.0 copy-done
  90.4 1.8 %basis.1 = bf16[1024,256]{1,0:T(8,128)(2,1)} custom-call(f32[1024,256]{1,0:T(8,128)S(1)} %copy-done, f32[256,256]{1,0:T(8,128)S(1)} %get-tuple-element.44.inverse_ref), custom_call_target="tpu_custom_call" | custom-call | flops 2147483648 | bytes 1048576 | tf_op jit(solution)/shard_map/basis/pallas_call | solution.py:315
  92.2 0.0 collective-permute-done.17
  92.2 0.8 convolution_multiply_fusion
  (19 shorter events, 0.4 us)
Async XLA Ops:
  15.0 6.0 %collective-permute-start = (f32[2,584,256]{2,1,0:T(8,128)}, f32[2,584,256]{2,1,0:T(8,128)S(1)}, u32[]{:S(2)}, u32[]{:S(2)}) collective-permute-start(f32[2,584,256]{2,1,0:T(8,128)} %get-tuple-element.29), channel_id=1, source_target_pairs={{0,16},{1,17},{2,18},{3,19},{4,20},{5,21},{6,22},{7,23},{8,24},{9,... | collective-permute-start | bytes 3588104 | tf_op jit(solution)/shard_map/ppermute | solution.py:331
  22.4 4.9 %copy-start.1 = (f32[2,584,256]{2,1,0:T(8,128)S(1)}, f32[2,584,256]{2,1,0:T(8,128)}, u32[]{:S(2)}) copy-start(f32[2,584,256]{2,1,0:T(8,128)} %get-tuple-element.26) | copy-start | bytes 3588100
  22.5 4.9 %collective-permute-start.1 = (f32[2,584,256]{2,1,0:T(8,128)}, f32[2,584,256]{2,1,0:T(8,128)}, u32[]{:S(2)}, u32[]{:S(2)}) collective-permute-start(f32[2,584,256]{2,1,0:T(8,128)} %get-tuple-element.30), channel_id=1, source_target_pairs={{0,16},{1,17},{2,18},{3,19},{4,20},{5,21},{6,22},{7,23},{8,24},{9,... | collective-permute-start | bytes 3588104 | tf_op jit(solution)/shard_map/ppermute | solution.py:331
  24.1 9.4 %collective-permute-start.3 = (f32[584,256]{1,0:T(8,128)}, f32[584,256]{1,0:T(8,128)S(1)}, u32[]{:S(2)}, u32[]{:S(2)}) collective-permute-start(f32[584,256]{1,0:T(8,128)} %get-tuple-element.49), channel_id=1, source_target_pairs={{0,1},{1,0},{2,3},{3,2},{4,5},{5,4},{6,7},{7,6},{8,9},{9,8},{10,11... | collective-permute-start | bytes 1794056 | tf_op jit(solution)/shard_map/ppermute | solution.py:331
  24.1 11.4 %collective-permute-start.2 = (f32[584,256]{1,0:T(8,128)}, f32[584,256]{1,0:T(8,128)}, u32[]{:S(2)}, u32[]{:S(2)}) collective-permute-start(f32[584,256]{1,0:T(8,128)} %get-tuple-element.50), channel_id=1, source_target_pairs={{0,3},{1,2},{2,1},{3,0},{4,7},{5,6},{6,5},{7,4},{8,11},{9,10},{10,... | collective-permute-start | bytes 1794056 | tf_op jit(solution)/shard_map/ppermute | solution.py:331
  25.5 11.3 %collective-permute-start.4 = (f32[72,256]{1,0:T(8,128)S(1)}, f32[72,256]{1,0:T(8,128)S(1)}, u32[]{:S(2)}, u32[]{:S(2)}) collective-permute-start(f32[72,256]{1,0:T(8,128)S(1)} %slice_bitcast_fusion.4), channel_id=1, source_target_pairs={{0,2},{1,3},{2,0},{3,1},{4,6},{5,7},{6,4},{7,5},{8,10},{9,11},{10,... | collective-permute-start | bytes 221192 | tf_op jit(solution)/shard_map/ppermute | solution.py:331
  36.9 7.6 %collective-permute-start.5 = (f32[328,256]{1,0:T(8,128)S(1)}, f32[328,256]{1,0:T(8,128)S(1)}, u32[]{:S(2)}, u32[]{:S(2)}) collective-permute-start(f32[328,256]{1,0:T(8,128)S(1)} %get-tuple-element.54), channel_id=1, source_target_pairs={{0,12},{1,13},{2,14},{3,15},{4,8},{5,9},{6,10},{7,11},{8,4},{9,5},... | collective-permute-start | bytes 1007624 | tf_op jit(solution)/shard_map/ppermute | solution.py:331
  38.3 6.3 %collective-permute-start.6 = (f32[328,256]{1,0:T(8,128)S(1)}, f32[328,256]{1,0:T(8,128)S(1)}, u32[]{:S(2)}, u32[]{:S(2)}) collective-permute-start(f32[328,256]{1,0:T(8,128)S(1)} %get-tuple-element.53), channel_id=1, source_target_pairs={{0,4},{1,5},{2,6},{3,7},{4,0},{5,1},{6,2},{7,3},{8,12},{9,13},{10,... | collective-permute-start | bytes 1007624 | tf_op jit(solution)/shard_map/ppermute | solution.py:331
  38.3 8.7 %collective-permute-start.10 = (f32[72,256]{1,0:T(8,128)S(1)}, f32[72,256]{1,0:T(8,128)S(1)}, u32[]{:S(2)}, u32[]{:S(2)}) collective-permute-start(f32[72,256]{1,0:T(8,128)S(1)} %fusion.3), channel_id=1, source_target_pairs={{0,8},{1,9},{2,10},{3,11},{4,12},{5,13},{6,14},{7,15},{8,0},{9,1},... | collective-permute-start | bytes 221192 | tf_op jit(solution)/shard_map/ppermute | solution.py:331
  44.7 8.0 %collective-permute-start.7 = (f32[2,128,256]{2,1,0:T(8,128)S(1)}, f32[2,128,256]{2,1,0:T(8,128)S(1)}, u32[]{:S(2)}, u32[]{:S(2)}) collective-permute-start(f32[2,128,256]{2,1,0:T(8,128)S(1)} %broadcast_select_fusion), channel_id=1, source_target_pairs={{0,2},{1,3},{2,0},{3,1},{4,6},{5,7},{6,4},{7,5},{8,10},{9,11},{10,... | collective-permute-start | bytes 786440 | tf_op jit(solution)/shard_map/ppermute | solution.py:331
  47.0 8.5 %collective-permute-start.11 = (f32[72,256]{1,0:T(8,128)S(1)}, f32[72,256]{1,0:T(8,128)S(1)}, u32[]{:S(2)}, u32[]{:S(2)}) collective-permute-start(f32[72,256]{1,0:T(8,128)S(1)} %fusion.2), channel_id=1, source_target_pairs={{0,224},{1,225},{2,226},{3,227},{4,228},{5,229},{6,230},{7,231},{8... | collective-permute-start | bytes 221192 | tf_op jit(solution)/shard_map/ppermute | solution.py:331
  52.8 6.5 %collective-permute-start.8 = (f32[128,256]{1,0:T(8,128)S(1)}, f32[128,256]{1,0:T(8,128)S(1)}, u32[]{:S(2)}, u32[]{:S(2)}) collective-permute-start(f32[128,256]{1,0:T(8,128)S(1)} %dynamic-slice_bitcast_fusion), channel_id=1, source_target_pairs={{0,8},{1,9},{2,10},{3,11},{4,12},{5,13},{6,14},{7,15},{8,0},{9,1},... | collective-permute-start | bytes 393224 | tf_op jit(solution)/shard_map/ppermute | solution.py:331
  55.5 3.8 %collective-permute-start.12 = (f32[72,256]{1,0:T(8,128)S(1)}, f32[72,256]{1,0:T(8,128)S(1)}, u32[]{:S(2)}, u32[]{:S(2)}) collective-permute-start(f32[72,256]{1,0:T(8,128)S(1)} %add.113), channel_id=1, source_target_pairs={{0,64},{1,65},{2,66},{3,67},{4,68},{5,69},{6,70},{7,71},{8,72},{9,... | collective-permute-start | bytes 221192 | tf_op jit(solution)/shard_map/ppermute | solution.py:331
  59.4 8.0 %collective-permute-start.13 = (f32[72,256]{1,0:T(8,128)S(1)}, f32[72,256]{1,0:T(8,128)S(1)}, u32[]{:S(2)}, u32[]{:S(2)}) collective-permute-start(f32[72,256]{1,0:T(8,128)S(1)} %add.114), channel_id=1, source_target_pairs={{0,32},{1,33},{2,34},{3,35},{4,36},{5,37},{6,38},{7,39},{8,40},{9,... | collective-permute-start | bytes 221192 | tf_op jit(solution)/shard_map/ppermute | solution.py:331
  60.5 11.9 %collective-permute-start.9 = (f32[128,256]{1,0:T(8,128)S(1)}, f32[128,256]{1,0:T(8,128)S(1)}, u32[]{:S(2)}, u32[]{:S(2)}) collective-permute-start(f32[128,256]{1,0:T(8,128)S(1)} %bitcast_add_fusion.2), channel_id=1, source_target_pairs={{0,32},{1,33},{2,34},{3,35},{4,36},{5,37},{6,38},{7,39},{8,40},{9,... | collective-permute-start | bytes 393224 | tf_op jit(solution)/shard_map/ppermute | solution.py:331
  67.4 5.9 %collective-permute-start.14 = (f32[72,256]{1,0:T(8,128)S(1)}, f32[72,256]{1,0:T(8,128)S(1)}, u32[]{:S(2)}, u32[]{:S(2)}) collective-permute-start(f32[72,256]{1,0:T(8,128)S(1)} %add.115), channel_id=1, source_target_pairs={{0,16},{1,17},{2,18},{3,19},{4,20},{5,21},{6,22},{7,23},{8,24},{9,... | collective-permute-start | bytes 221192 | tf_op jit(solution)/shard_map/ppermute | solution.py:331
  73.3 5.5 %collective-permute-start.15 = (f32[128,256]{1,0:T(8,128)S(1)}, f32[128,256]{1,0:T(8,128)S(1)}, u32[]{:S(2)}, u32[]{:S(2)}) collective-permute-start(f32[128,256]{1,0:T(8,128)S(1)} %add.109), channel_id=1, source_target_pairs={{0,64},{1,65},{2,66},{3,67},{4,68},{5,69},{6,70},{7,71},{8,72},{9,... | collective-permute-start | bytes 393224 | tf_op jit(solution)/shard_map/ppermute | solution.py:331
  78.8 11.6 %copy-start = (f32[1024,256]{1,0:T(8,128)S(1)}, f32[1024,256]{1,0:T(8,128)}, u32[]{:S(2)}) copy-start(f32[1024,256]{1,0:T(8,128)} %get-tuple-element.25.sketched_ref) | copy-start | bytes 3145732
  78.8 8.9 %collective-permute-start.16 = (f32[128,256]{1,0:T(8,128)S(1)}, f32[128,256]{1,0:T(8,128)S(1)}, u32[]{:S(2)}, u32[]{:S(2)}) collective-permute-start(f32[128,256]{1,0:T(8,128)S(1)} %add.116), channel_id=1, source_target_pairs={{0,224},{1,225},{2,226},{3,227},{4,228},{5,229},{6,230},{7,231},{8... | collective-permute-start | bytes 393224 | tf_op jit(solution)/shard_map/ppermute | solution.py:331
  87.7 4.5 %collective-permute-start.17 = (f32[128,256]{1,0:T(8,128)S(1)}, f32[128,256]{1,0:T(8,128)S(1)}, u32[]{:S(2)}, u32[]{:S(2)}) collective-permute-start(f32[128,256]{1,0:T(8,128)S(1)} %add.117), channel_id=1, source_target_pairs={{0,16},{1,17},{2,18},{3,19},{4,20},{5,21},{6,22},{7,23},{8,24},{9,... | collective-permute-start | bytes 393224 | tf_op jit(solution)/shard_map/ppermute | solution.py:331

commit v3 on v2

--- a/solution.py
+++ b/solution.py
@@ -332,7 +332,7 @@
 
 
 X1, X2, Y1, Y2 = (0, 1), (0, 2), (0, 4), (0, 8)
-Z1, Z2, Z7 = (2, 0), (4, 0), (14, 0)
+Z1, Z2, Z6 = (2, 0), (4, 0), (12, 0)
 CORE = ((1, 0), (1, 0))
 
 
@@ -366,11 +366,12 @@
     half = rank // 2
     rows = SIDE * half
 
-    message = send + trade(away_send, CORE)
-    keep = keep + trade(after(away_keep, message), CORE)
+    got = trade(away_send, CORE)
+    message = [send[side] + got[side] for side in range(2)]
+    keep = keep + trade(after(away_keep, message[0]), CORE)
     one = keep[0] + trade(message[0], (X1, Y1))
     three = keep[1] + trade(message[1], (X3, Y3))
-    piece = one[rows:] + (trade(message[0, rows:], (X2, Y2)) + three[rows:])
+    piece = one[rows:] + (trade(message[0][rows:], (X2, Y2)) + three[rows:])
     terms = [part[:rows].reshape(2, 2, half, -1) for part in (one, three)]
     parts = [halves(term, inner % 2, 1) for term in terms]
     one, piece_1 = trade_both(parts[0][1], piece, (Y1, X1))
@@ -379,7 +380,7 @@
     low, high = (part[0] + got for part, got in zip(parts, (one, three)))
     upper = outer // 2 == 1
     term = jnp.where(upper, high, low) + trade(jnp.where(upper, low, high), (X2, Y2))
-    piece = piece + trade(piece, (Z7, Z7))
+    piece = piece + trade(piece, (Z6, Z6))
     keep, send = halves(term, inner // 2, 0)
     term = keep + trade(send, (Y2, X2))
     piece = piece + trade(piece, (Z2, Z1))
@@ -387,14 +388,14 @@
 
     other = trade(piece, CORE)
     corner, mixed = jnp.where(core == 0, piece, other), jnp.where(core == 0, other, piece)
-    block = 64
+    block = 128
     term = term + trade(term, (Z1, Z2))
     term, corner, mixed = lax.optimization_barrier((term, corner, mixed))
     state = factorize_first(corner, mixed, rank, block)
     term = term + trade(term, (Z2, Z1))
     term, *state = lax.optimization_barrier((term, *state))
     factor, inverse = factorize_second(*state, block)
-    term = term + trade(term, (Z7, Z7))
+    term = term + trade(term, (Z6, Z6))
     term, factor, inverse = lax.optimization_barrier((term, factor, inverse))
     basis = basis_of(sketched, inverse)
     summed = order(core, term, trade(term, CORE)).reshape(rank, -1)

time: 93.3 us -> 92.7 us (level)
  starting transfers between devices: 34.3 us -> 36.3 us
  local copies, waits for them, and re-layouts: 1.33 us -> 0.18 us
    ppermute x18, starting transfers between devices: 34.3 us -> 36.3 us  [trade(): return lax.ppermute(value, ('gx', 'gy'), pairs)]
    squeeze x2 -> x0, local copies, waits for them, and re-layouts: 1.15 us -> none  [the longest x1 1.14 us: body(): one = keep[0] + trade(message[0], (X1, Y1))]
  transfers between devices with their start and end apart: 18 -> 18, of which waited for: 8 -> 10; matrix products, arithmetic and copies ran while one was open for 5% -> 2% of each run, Pallas kernels for 13% -> 13%
where the time goes in v3:
time: 92.7 us; the launch traced here: 92.6 us
  starting transfers between devices  36.3 us (39%)
  Pallas kernels  26.1 us (28%)
  waiting for transfers between devices  24 us (26%)
  other arithmetic  4.29 us (5%)
    ppermute x18, starting transfers between devices, trade(): return lax.ppermute(value, ('gx', 'gy'), pairs)  36.3 us
    ppermute x18, waiting for transfers between devices, trade(): return lax.ppermute(value, ('gx', 'gy'), pairs)  24 us
    pallas_call x1, Pallas kernels, front(): pl.pallas_call(functools.partial(front_kernel, scale=scale), in_specs=[hb...  14.3 us
    pallas_call x1, Pallas kernels, factorize_first(): pl.pallas_call(functools.partial(first_kernel, block=block), out_shape=[j...  5.16 us
    pallas_call x1, Pallas kernels, factorize_second(): pl.pallas_call(functools.partial(second_kernel, block=block), out_shape=[...  4.83 us
    add x1, other arithmetic, body(): message = [send[side] + got[side] for side in range(2)]  2.33 us
  transfers between devices with their start and end apart: 18, of which 10 were waited for; matrix products, arithmetic and copies ran while one was open for 2% of the time, Pallas kernels for 13%

profile of v3, /device:TPU:1, one launch (start us, length us, event | category | flops | bytes accessed | tf_op | source)
XLA Modules:
  0.0 92.6 jit_solution(10730205747890418497)
XLA Ops:
  0.6 14.3 %front.1 = (f32[1024,256]{1,0:T(8,128)}, f32[2,584,256]{2,1,0:T(8,128)}, f32[2,584,256]{2,1,0:T(8,128)}, f32[2,584,256]{2,1,0:T(8,128)}, f32[2,584,256]{2,1,0:T(8,128)}) custom-call(bf16[1024,4096]{1,0:T(8,128)(2,1)} %rows_hbm.1, bf16[4096,256]{1,0:T(8,128)(2,1)} %sketch_hbm.1), custom_call_target="tpu_custom_call" | custom-call | flops 6442450944 | bytes 16777216 | tf_op jit(solution)/shard_map/front/pallas_call | solution.py:133
  15.0 3.3 %collective-permute-start = (f32[2,584,256]{2,1,0:T(8,128)}, f32[2,584,256]{2,1,0:T(8,128)S(1)}, u32[]{:S(2)}, u32[]{:S(2)}) collective-permute-start(f32[2,584,256]{2,1,0:T(8,128)} %get-tuple-element.29), channel_id=1, source_target_pairs={{0,16},{1,17},{2,18},{3,19},{4,20},{5,21},{6,22},{7,23},{8,24},{9,... | collective-permute-start | bytes 3588104 | tf_op jit(solution)/shard_map/ppermute | solution.py:331
  18.3 2.7 %collective-permute-done = f32[2,584,256]{2,1,0:T(8,128)S(1)} collective-permute-done((f32[2,584,256]{2,1,0:T(8,128)}, f32[2,584,256]{2,1,0:T(8,128)S(1)}, u32[]{:S(2)}, u32[]{:S(2)}) %collective-permute-start) | collective-permute-done | bytes 1196064 | tf_op jit(solution)/shard_map/ppermute | solution.py:331
  21.0 0.0 copy-start.1
  21.0 2.3 %fusion.1 = (f32[584,256]{1,0:T(8,128)}, f32[1,584,256]{2,1,0:T(8,128)S(1)}) fusion(f32[2,584,256]{2,1,0:T(8,128)S(1)} %collective-permute-done, f32[2,584,256]{2,1,0:T(8,128)} %get-tuple-element.28), kind=kLoop, calls=%fused_computation.4 | loop fusion | flops 299008 | bytes 3588096 | tf_op jit(solution)/shard_map/add | solution.py:370
  23.3 0.4 collective-permute-start.1
  23.7 0.0 collective-permute-start.3
  23.7 1.5 %collective-permute-start.2 = (f32[584,256]{1,0:T(8,128)}, f32[584,256]{1,0:T(8,128)}, u32[]{:S(2)}, u32[]{:S(2)}) collective-permute-start(f32[584,256]{1,0:T(8,128)} %get-tuple-element.47), channel_id=1, source_target_pairs={{0,3},{1,2},{2,1},{3,0},{4,7},{5,6},{6,5},{7,4},{8,11},{9,10},{10,... | collective-permute-start | bytes 1794056 | tf_op jit(solution)/shard_map/ppermute | solution.py:331
  25.2 1.8 %collective-permute-start.4 = (f32[72,256]{1,0:T(8,128)S(1)}, f32[72,256]{1,0:T(8,128)S(1)}, u32[]{:S(2)}, u32[]{:S(2)}) collective-permute-start(f32[72,256]{1,0:T(8,128)S(1)} %slice_bitcast_fusion.2), channel_id=1, source_target_pairs={{0,2},{1,3},{2,0},{3,1},{4,6},{5,7},{6,4},{7,5},{8,10},{9,11},{10,... | collective-permute-start | bytes 221192 | tf_op jit(solution)/shard_map/ppermute | solution.py:331
  27.0 0.0 collective-permute-done.1
  27.0 0.0 copy-done.1
  27.0 0.2 add.105
  27.1 5.8 %collective-permute-done.3 = f32[584,256]{1,0:T(8,128)} collective-permute-done((f32[584,256]{1,0:T(8,128)S(1)}, f32[584,256]{1,0:T(8,128)}, u32[]{:S(2)}, u32[]{:S(2)}) %collective-permute-start.3) | collective-permute-done | bytes 598048 | tf_op jit(solution)/shard_map/ppermute | solution.py:331
  32.9 2.2 %collective-permute-done.2 = f32[584,256]{1,0:T(8,128)} collective-permute-done((f32[584,256]{1,0:T(8,128)}, f32[584,256]{1,0:T(8,128)}, u32[]{:S(2)}, u32[]{:S(2)}) %collective-permute-start.2) | collective-permute-done | bytes 598048 | tf_op jit(solution)/shard_map/ppermute | solution.py:331
  35.2 1.4 %fusion = (f32[584,256]{1,0:T(8,128)S(1)}, f32[584,256]{1,0:T(8,128)S(1)}) fusion(f32[584,256]{1,0:T(8,128)} %collective-permute-done.3, f32[2,584,256]{2,1,0:T(8,128)S(1)} %add.105, f32[584,256]{1,0:T(8,128)} %collective-permute-done.2), kind=kLoop, calls=%fused_computation.2 | loop fusion | flops 299008 | bytes 3588096 | tf_op jit(solution)/shard_map/add | solution.py:372
  36.7 0.0 collective-permute-done.4
  36.8 2.1 %collective-permute-start.5 = (f32[328,256]{1,0:T(8,128)S(1)}, f32[328,256]{1,0:T(8,128)S(1)}, u32[]{:S(2)}, u32[]{:S(2)}) collective-permute-start(f32[328,256]{1,0:T(8,128)S(1)} %get-tuple-element.54), channel_id=1, source_target_pairs={{0,12},{1,13},{2,14},{3,15},{4,8},{5,9},{6,10},{7,11},{8,4},{9,5},... | collective-permute-start | bytes 1007624 | tf_op jit(solution)/shard_map/ppermute | solution.py:331
  38.9 0.0 collective-permute-start.6
  38.9 1.8 %collective-permute-start.10 = (f32[72,256]{1,0:T(8,128)S(1)}, f32[72,256]{1,0:T(8,128)S(1)}, u32[]{:S(2)}, u32[]{:S(2)}) collective-permute-start(f32[72,256]{1,0:T(8,128)S(1)} %fusion.4), channel_id=1, source_target_pairs={{0,8},{1,9},{2,10},{3,11},{4,12},{5,13},{6,14},{7,15},{8,0},{9,1},... | collective-permute-start | bytes 221192 | tf_op jit(solution)/shard_map/ppermute | solution.py:331
  40.7 3.7 %collective-permute-done.5 = f32[328,256]{1,0:T(8,128)S(1)} collective-permute-done((f32[328,256]{1,0:T(8,128)S(1)}, f32[328,256]{1,0:T(8,128)S(1)}, u32[]{:S(2)}, u32[]{:S(2)}) %collective-permute-start.5) | collective-permute-done | bytes 335904 | tf_op jit(solution)/shard_map/ppermute | solution.py:331
  44.4 0.8 collective-permute-done.6
  45.2 0.1 broadcast_select_fusion
  45.3 1.5 %collective-permute-start.7 = (f32[2,128,256]{2,1,0:T(8,128)S(1)}, f32[2,128,256]{2,1,0:T(8,128)S(1)}, u32[]{:S(2)}, u32[]{:S(2)}) collective-permute-start(f32[2,128,256]{2,1,0:T(8,128)S(1)} %broadcast_select_fusion), channel_id=1, source_target_pairs={{0,2},{1,3},{2,0},{3,1},{4,6},{5,7},{6,4},{7,5},{8,10},{9,11},{10,... | collective-permute-start | bytes 786440 | tf_op jit(solution)/shard_map/ppermute | solution.py:331
  46.8 0.0 collective-permute-done.10
  46.8 6.1 %collective-permute-start.11 = (f32[72,256]{1,0:T(8,128)S(1)}, f32[72,256]{1,0:T(8,128)S(1)}, u32[]{:S(2)}, u32[]{:S(2)}) collective-permute-start(f32[72,256]{1,0:T(8,128)S(1)} %fusion.3), channel_id=1, source_target_pairs={{0,192},{1,193},{2,194},{3,195},{4,196},{5,197},{6,198},{7,199},{8... | collective-permute-start | bytes 221192 | tf_op jit(solution)/shard_map/ppermute | solution.py:331
  52.9 0.0 collective-permute-done.7
  53.0 0.1 select_add_fusion
  53.1 0.5 collective-permute-start.8
  53.6 1.4 %collective-permute-done.11 = f32[72,256]{1,0:T(8,128)S(1)} collective-permute-done((f32[72,256]{1,0:T(8,128)S(1)}, f32[72,256]{1,0:T(8,128)S(1)}, u32[]{:S(2)}, u32[]{:S(2)}) %collective-permute-start.11) | collective-permute-done | bytes 73760 | tf_op jit(solution)/shard_map/ppermute | solution.py:331
  55.0 1.6 %collective-permute-start.12 = (f32[72,256]{1,0:T(8,128)S(1)}, f32[72,256]{1,0:T(8,128)S(1)}, u32[]{:S(2)}, u32[]{:S(2)}) collective-permute-start(f32[72,256]{1,0:T(8,128)S(1)} %add.125), channel_id=1, source_target_pairs={{0,64},{1,65},{2,66},{3,67},{4,68},{5,69},{6,70},{7,71},{8,72},{9,... | collective-permute-start | bytes 221192 | tf_op jit(solution)/shard_map/ppermute | solution.py:331
  56.6 2.3 %collective-permute-done.12 = f32[72,256]{1,0:T(8,128)S(1)} collective-permute-done((f32[72,256]{1,0:T(8,128)S(1)}, f32[72,256]{1,0:T(8,128)S(1)}, u32[]{:S(2)}, u32[]{:S(2)}) %collective-permute-start.12) | collective-permute-done | bytes 73760 | tf_op jit(solution)/shard_map/ppermute | solution.py:331
  58.9 0.0 collective-permute-done.8
  59.0 1.8 %collective-permute-start.13 = (f32[72,256]{1,0:T(8,128)S(1)}, f32[72,256]{1,0:T(8,128)S(1)}, u32[]{:S(2)}, u32[]{:S(2)}) collective-permute-start(f32[72,256]{1,0:T(8,128)S(1)} %add.126), channel_id=1, source_target_pairs={{0,32},{1,33},{2,34},{3,35},{4,36},{5,37},{6,38},{7,39},{8,40},{9,... | collective-permute-start | bytes 221192 | tf_op jit(solution)/shard_map/ppermute | solution.py:331
  60.8 0.7 collective-permute-start.9
  61.4 4.1 %collective-permute-done.13 = f32[72,256]{1,0:T(8,128)S(1)} collective-permute-done((f32[72,256]{1,0:T(8,128)S(1)}, f32[72,256]{1,0:T(8,128)S(1)}, u32[]{:S(2)}, u32[]{:S(2)}) %collective-permute-start.13) | collective-permute-done | bytes 73760 | tf_op jit(solution)/shard_map/ppermute | solution.py:331
  65.5 5.0 %collective-permute-start.14 = (f32[72,256]{1,0:T(8,128)S(1)}, f32[72,256]{1,0:T(8,128)S(1)}, u32[]{:S(2)}, u32[]{:S(2)}) collective-permute-start(f32[72,256]{1,0:T(8,128)S(1)} %add.127), channel_id=1, source_target_pairs={{0,16},{1,17},{2,18},{3,19},{4,20},{5,21},{6,22},{7,23},{8,24},{9,... | collective-permute-start | bytes 221192 | tf_op jit(solution)/shard_map/ppermute | solution.py:331
  70.5 0.0 collective-permute-done.9
  70.5 0.9 collective-permute-done.14
  71.4 1.0 %collective-permute-start.15 = (f32[128,256]{1,0:T(8,128)S(1)}, f32[128,256]{1,0:T(8,128)S(1)}, u32[]{:S(2)}, u32[]{:S(2)}) collective-permute-start(f32[128,256]{1,0:T(8,128)S(1)} %add.121), channel_id=1, source_target_pairs={{0,64},{1,65},{2,66},{3,67},{4,68},{5,69},{6,70},{7,71},{8,72},{9,... | collective-permute-start | bytes 393224 | tf_op jit(solution)/shard_map/ppermute | solution.py:331
  72.5 5.2 %factorize_first.1 = (f32[256,256]{1,0:T(8,128)S(1)}, f32[256,128]{1,0:T(8,128)S(1)}, f32[8,256]{1,0:T(8,128)S(1)}) custom-call(f32[72,256]{1,0:T(8,128)S(1)} %get-tuple-element.33.corner_ref, f32[72,256]{1,0:T(8,128)S(1)} %get-tuple-element.34.mixed_ref), custom_call_target="tpu_custom_call" | custom-call | flops 6442450944 | bytes 1048576 | tf_op jit(solution)/shard_map/factorize_first/pallas_call | solution.py:285
  77.6 0.0 collective-permute-done.15
  77.7 0.0 copy-start
  77.7 5.6 %collective-permute-start.16 = (f32[128,256]{1,0:T(8,128)S(1)}, f32[128,256]{1,0:T(8,128)S(1)}, u32[]{:S(2)}, u32[]{:S(2)}) collective-permute-start(f32[128,256]{1,0:T(8,128)S(1)} %add.128), channel_id=1, source_target_pairs={{0,192},{1,193},{2,194},{3,195},{4,196},{5,197},{6,198},{7,199},{8... | collective-permute-start | bytes 393224 | tf_op jit(solution)/shard_map/ppermute | solution.py:331
  83.3 4.8 %factorize_second.1 = (f32[256,256]{1,0:T(8,128)}, f32[256,256]{1,0:T(8,128)S(1)}) custom-call(f32[256,256]{1,0:T(8,128)S(1)} %get-tuple-element.39.state_ref, f32[256,128]{1,0:T(8,128)S(1)} %get-tuple-element.40.upper_ref, f32[8,256]{1,0:T(8,128)S(1)} %get-tuple-element.41.scales_ref), custom_call_target="tpu_custom_call" | custom-call | flops 6442450944 | bytes 1048576 | tf_op jit(solution)/shard_map/factorize_second/pallas_call | solution.py:300
  88.1 0.1 collective-permute-done.16
  88.2 1.7 %collective-permute-start.17 = (f32[128,256]{1,0:T(8,128)S(1)}, f32[128,256]{1,0:T(8,128)S(1)}, u32[]{:S(2)}, u32[]{:S(2)}) collective-permute-start(f32[128,256]{1,0:T(8,128)S(1)} %add.129), channel_id=1, source_target_pairs={{0,16},{1,17},{2,18},{3,19},{4,20},{5,21},{6,22},{7,23},{8,24},{9,... | collective-permute-start | bytes 393224 | tf_op jit(solution)/shard_map/ppermute | solution.py:331
  89.9 0.0 copy-done
  89.9 1.8 %basis.1 = bf16[1024,256]{1,0:T(8,128)(2,1)} custom-call(f32[1024,256]{1,0:T(8,128)S(1)} %copy-done, f32[256,256]{1,0:T(8,128)S(1)} %get-tuple-element.44.inverse_ref), custom_call_target="tpu_custom_call" | custom-call | flops 2147483648 | bytes 1048576 | tf_op jit(solution)/shard_map/basis/pallas_call | solution.py:315
  91.7 0.0 collective-permute-done.17
  91.8 0.8 convolution_multiply_fusion
  (19 shorter events, 0.4 us)
Async XLA Ops:
  15.0 6.0 %collective-permute-start = (f32[2,584,256]{2,1,0:T(8,128)}, f32[2,584,256]{2,1,0:T(8,128)S(1)}, u32[]{:S(2)}, u32[]{:S(2)}) collective-permute-start(f32[2,584,256]{2,1,0:T(8,128)} %get-tuple-element.29), channel_id=1, source_target_pairs={{0,16},{1,17},{2,18},{3,19},{4,20},{5,21},{6,22},{7,23},{8,24},{9,... | collective-permute-start | bytes 3588104 | tf_op jit(solution)/shard_map/ppermute | solution.py:331
  21.0 6.0 %copy-start.1 = (f32[2,584,256]{2,1,0:T(8,128)S(1)}, f32[2,584,256]{2,1,0:T(8,128)}, u32[]{:S(2)}) copy-start(f32[2,584,256]{2,1,0:T(8,128)} %get-tuple-element.26) | copy-start | bytes 3588100
  23.3 3.6 %collective-permute-start.1 = (f32[2,584,256]{2,1,0:T(8,128)}, f32[2,584,256]{2,1,0:T(8,128)S(1)}, u32[]{:S(2)}, u32[]{:S(2)}) collective-permute-start(f32[2,584,256]{2,1,0:T(8,128)} %get-tuple-element.30), channel_id=1, source_target_pairs={{0,16},{1,17},{2,18},{3,19},{4,20},{5,21},{6,22},{7,23},{8,24},{9,... | collective-permute-start | bytes 3588104 | tf_op jit(solution)/shard_map/ppermute | solution.py:331
  23.7 9.2 %collective-permute-start.3 = (f32[584,256]{1,0:T(8,128)S(1)}, f32[584,256]{1,0:T(8,128)}, u32[]{:S(2)}, u32[]{:S(2)}) collective-permute-start(f32[584,256]{1,0:T(8,128)S(1)} %bitcast.54), channel_id=1, source_target_pairs={{0,1},{1,0},{2,3},{3,2},{4,5},{5,4},{6,7},{7,6},{8,9},{9,8},{10,11... | collective-permute-start | bytes 1794056 | tf_op jit(solution)/shard_map/ppermute | solution.py:331
  23.7 11.4 %collective-permute-start.2 = (f32[584,256]{1,0:T(8,128)}, f32[584,256]{1,0:T(8,128)}, u32[]{:S(2)}, u32[]{:S(2)}) collective-permute-start(f32[584,256]{1,0:T(8,128)} %get-tuple-element.47), channel_id=1, source_target_pairs={{0,3},{1,2},{2,1},{3,0},{4,7},{5,6},{6,5},{7,4},{8,11},{9,10},{10,... | collective-permute-start | bytes 1794056 | tf_op jit(solution)/shard_map/ppermute | solution.py:331
  25.2 11.5 %collective-permute-start.4 = (f32[72,256]{1,0:T(8,128)S(1)}, f32[72,256]{1,0:T(8,128)S(1)}, u32[]{:S(2)}, u32[]{:S(2)}) collective-permute-start(f32[72,256]{1,0:T(8,128)S(1)} %slice_bitcast_fusion.2), channel_id=1, source_target_pairs={{0,2},{1,3},{2,0},{3,1},{4,6},{5,7},{6,4},{7,5},{8,10},{9,11},{10,... | collective-permute-start | bytes 221192 | tf_op jit(solution)/shard_map/ppermute | solution.py:331
  36.8 7.6 %collective-permute-start.5 = (f32[328,256]{1,0:T(8,128)S(1)}, f32[328,256]{1,0:T(8,128)S(1)}, u32[]{:S(2)}, u32[]{:S(2)}) collective-permute-start(f32[328,256]{1,0:T(8,128)S(1)} %get-tuple-element.54), channel_id=1, source_target_pairs={{0,12},{1,13},{2,14},{3,15},{4,8},{5,9},{6,10},{7,11},{8,4},{9,5},... | collective-permute-start | bytes 1007624 | tf_op jit(solution)/shard_map/ppermute | solution.py:331
  38.9 6.3 %collective-permute-start.6 = (f32[328,256]{1,0:T(8,128)S(1)}, f32[328,256]{1,0:T(8,128)S(1)}, u32[]{:S(2)}, u32[]{:S(2)}) collective-permute-start(f32[328,256]{1,0:T(8,128)S(1)} %get-tuple-element.53), channel_id=1, source_target_pairs={{0,4},{1,5},{2,6},{3,7},{4,0},{5,1},{6,2},{7,3},{8,12},{9,13},{10,... | collective-permute-start | bytes 1007624 | tf_op jit(solution)/shard_map/ppermute | solution.py:331
  38.9 7.9 %collective-permute-start.10 = (f32[72,256]{1,0:T(8,128)S(1)}, f32[72,256]{1,0:T(8,128)S(1)}, u32[]{:S(2)}, u32[]{:S(2)}) collective-permute-start(f32[72,256]{1,0:T(8,128)S(1)} %fusion.4), channel_id=1, source_target_pairs={{0,8},{1,9},{2,10},{3,11},{4,12},{5,13},{6,14},{7,15},{8,0},{9,1},... | collective-permute-start | bytes 221192 | tf_op jit(solution)/shard_map/ppermute | solution.py:331
  45.3 7.6 %collective-permute-start.7 = (f32[2,128,256]{2,1,0:T(8,128)S(1)}, f32[2,128,256]{2,1,0:T(8,128)S(1)}, u32[]{:S(2)}, u32[]{:S(2)}) collective-permute-start(f32[2,128,256]{2,1,0:T(8,128)S(1)} %broadcast_select_fusion), channel_id=1, source_target_pairs={{0,2},{1,3},{2,0},{3,1},{4,6},{5,7},{6,4},{7,5},{8,10},{9,11},{10,... | collective-permute-start | bytes 786440 | tf_op jit(solution)/shard_map/ppermute | solution.py:331
  46.8 8.2 %collective-permute-start.11 = (f32[72,256]{1,0:T(8,128)S(1)}, f32[72,256]{1,0:T(8,128)S(1)}, u32[]{:S(2)}, u32[]{:S(2)}) collective-permute-start(f32[72,256]{1,0:T(8,128)S(1)} %fusion.3), channel_id=1, source_target_pairs={{0,192},{1,193},{2,194},{3,195},{4,196},{5,197},{6,198},{7,199},{8... | collective-permute-start | bytes 221192 | tf_op jit(solution)/shard_map/ppermute | solution.py:331
  53.1 5.9 %collective-permute-start.8 = (f32[128,256]{1,0:T(8,128)S(1)}, f32[128,256]{1,0:T(8,128)S(1)}, u32[]{:S(2)}, u32[]{:S(2)}) collective-permute-start(f32[128,256]{1,0:T(8,128)S(1)} %dynamic-slice_bitcast_fusion), channel_id=1, source_target_pairs={{0,8},{1,9},{2,10},{3,11},{4,12},{5,13},{6,14},{7,15},{8,0},{9,1},... | collective-permute-start | bytes 393224 | tf_op jit(solution)/shard_map/ppermute | solution.py:331
  55.0 3.9 %collective-permute-start.12 = (f32[72,256]{1,0:T(8,128)S(1)}, f32[72,256]{1,0:T(8,128)S(1)}, u32[]{:S(2)}, u32[]{:S(2)}) collective-permute-start(f32[72,256]{1,0:T(8,128)S(1)} %add.125), channel_id=1, source_target_pairs={{0,64},{1,65},{2,66},{3,67},{4,68},{5,69},{6,70},{7,71},{8,72},{9,... | collective-permute-start | bytes 221192 | tf_op jit(solution)/shard_map/ppermute | solution.py:331
  59.0 6.5 %collective-permute-start.13 = (f32[72,256]{1,0:T(8,128)S(1)}, f32[72,256]{1,0:T(8,128)S(1)}, u32[]{:S(2)}, u32[]{:S(2)}) collective-permute-start(f32[72,256]{1,0:T(8,128)S(1)} %add.126), channel_id=1, source_target_pairs={{0,32},{1,33},{2,34},{3,35},{4,36},{5,37},{6,38},{7,39},{8,40},{9,... | collective-permute-start | bytes 221192 | tf_op jit(solution)/shard_map/ppermute | solution.py:331
  60.8 9.7 %collective-permute-start.9 = (f32[128,256]{1,0:T(8,128)S(1)}, f32[128,256]{1,0:T(8,128)S(1)}, u32[]{:S(2)}, u32[]{:S(2)}) collective-permute-start(f32[128,256]{1,0:T(8,128)S(1)} %bitcast_add_fusion.2), channel_id=1, source_target_pairs={{0,32},{1,33},{2,34},{3,35},{4,36},{5,37},{6,38},{7,39},{8,40},{9,... | collective-permute-start | bytes 393224 | tf_op jit(solution)/shard_map/ppermute | solution.py:331
  65.5 5.9 %collective-permute-start.14 = (f32[72,256]{1,0:T(8,128)S(1)}, f32[72,256]{1,0:T(8,128)S(1)}, u32[]{:S(2)}, u32[]{:S(2)}) collective-permute-start(f32[72,256]{1,0:T(8,128)S(1)} %add.127), channel_id=1, source_target_pairs={{0,16},{1,17},{2,18},{3,19},{4,20},{5,21},{6,22},{7,23},{8,24},{9,... | collective-permute-start | bytes 221192 | tf_op jit(solution)/shard_map/ppermute | solution.py:331
  71.4 6.2 %collective-permute-start.15 = (f32[128,256]{1,0:T(8,128)S(1)}, f32[128,256]{1,0:T(8,128)S(1)}, u32[]{:S(2)}, u32[]{:S(2)}) collective-permute-start(f32[128,256]{1,0:T(8,128)S(1)} %add.121), channel_id=1, source_target_pairs={{0,64},{1,65},{2,66},{3,67},{4,68},{5,69},{6,70},{7,71},{8,72},{9,... | collective-permute-start | bytes 393224 | tf_op jit(solution)/shard_map/ppermute | solution.py:331
  77.7 12.2 %copy-start = (f32[1024,256]{1,0:T(8,128)S(1)}, f32[1024,256]{1,0:T(8,128)}, u32[]{:S(2)}) copy-start(f32[1024,256]{1,0:T(8,128)} %get-tuple-element.25.sketched_ref) | copy-start | bytes 3145732
  77.7 10.5 %collective-permute-start.16 = (f32[128,256]{1,0:T(8,128)S(1)}, f32[128,256]{1,0:T(8,128)S(1)}, u32[]{:S(2)}, u32[]{:S(2)}) collective-permute-start(f32[128,256]{1,0:T(8,128)S(1)} %add.128), channel_id=1, source_target_pairs={{0,192},{1,193},{2,194},{3,195},{4,196},{5,197},{6,198},{7,199},{8... | collective-permute-start | bytes 393224 | tf_op jit(solution)/shard_map/ppermute | solution.py:331
  88.2 3.5 %collective-permute-start.17 = (f32[128,256]{1,0:T(8,128)S(1)}, f32[128,256]{1,0:T(8,128)S(1)}, u32[]{:S(2)}, u32[]{:S(2)}) collective-permute-start(f32[128,256]{1,0:T(8,128)S(1)} %add.129), channel_id=1, source_target_pairs={{0,16},{1,17},{2,18},{3,19},{4,20},{5,21},{6,22},{7,23},{8,24},{9,... | collective-permute-start | bytes 393224 | tf_op jit(solution)/shard_map/ppermute | solution.py:331

commit v4 on v3

--- a/solution.py
+++ b/solution.py
@@ -366,12 +366,11 @@
     half = rank // 2
     rows = SIDE * half
 
-    got = trade(away_send, CORE)
-    message = [send[side] + got[side] for side in range(2)]
-    keep = keep + trade(after(away_keep, message[0]), CORE)
+    message = send + trade(away_send, CORE)
+    keep = keep + trade(after(away_keep, message), CORE)
     one = keep[0] + trade(message[0], (X1, Y1))
     three = keep[1] + trade(message[1], (X3, Y3))
-    piece = one[rows:] + (trade(message[0][rows:], (X2, Y2)) + three[rows:])
+    piece = one[rows:] + (trade(message[0, rows:], (X2, Y2)) + three[rows:])
     terms = [part[:rows].reshape(2, 2, half, -1) for part in (one, three)]
     parts = [halves(term, inner % 2, 1) for term in terms]
     one, piece_1 = trade_both(parts[0][1], piece, (Y1, X1))

time: 92.7 us -> 93.2 us (level)
  local copies, waits for them, and re-layouts: 0.18 us -> 1.33 us
    squeeze x0 -> x2, local copies, waits for them, and re-layouts: none -> 1.15 us  [the longest x1 1.14 us: body(): one = keep[0] + trade(message[0], (X1, Y1))]
  transfers between devices with their start and end apart: 18 -> 18, of which waited for: 10 -> 9; matrix products, arithmetic and copies ran while one was open for 2% -> 5% of each run, Pallas kernels for 13% -> 13%
where the time goes in v4:
time: 93.2 us; the launch traced here: 93 us
  starting transfers between devices  35.7 us (38%)
  Pallas kernels  26.1 us (28%)
  waiting for transfers between devices  23.6 us (25%)
  other arithmetic  4.49 us (5%)
  local copies, waits for them, and re-layouts  1.33 us (1%)
    ppermute x18, starting transfers between devices, trade(): return lax.ppermute(value, ('gx', 'gy'), pairs)  35.7 us
    ppermute x18, waiting for transfers between devices, trade(): return lax.ppermute(value, ('gx', 'gy'), pairs)  23.6 us
    pallas_call x1, Pallas kernels, front(): pl.pallas_call(functools.partial(front_kernel, scale=scale), in_specs=[hb...  14.3 us
    pallas_call x1, Pallas kernels, factorize_first(): pl.pallas_call(functools.partial(first_kernel, block=block), out_shape=[j...  5.16 us
    pallas_call x1, Pallas kernels, factorize_second(): pl.pallas_call(functools.partial(second_kernel, block=block), out_shape=[...  4.83 us
  transfers between devices with their start and end apart: 18, of which 9 were waited for; matrix products, arithmetic and copies ran while one was open for 5% of the time, Pallas kernels for 13%

profile of v4, /device:TPU:1, one launch (start us, length us, event | category | flops | bytes accessed | tf_op | source)
XLA Modules:
  0.0 93.0 jit_solution(16850704613333475172)
XLA Ops:
  0.6 14.3 %front.1 = (f32[1024,256]{1,0:T(8,128)}, f32[2,584,256]{2,1,0:T(8,128)}, f32[2,584,256]{2,1,0:T(8,128)}, f32[2,584,256]{2,1,0:T(8,128)}, f32[2,584,256]{2,1,0:T(8,128)}) custom-call(bf16[1024,4096]{1,0:T(8,128)(2,1)} %rows_hbm.1, bf16[4096,256]{1,0:T(8,128)(2,1)} %sketch_hbm.1), custom_call_target="tpu_custom_call" | custom-call | flops 6442450944 | bytes 16777216 | tf_op jit(solution)/shard_map/front/pallas_call | solution.py:133
  15.0 3.3 %collective-permute-start = (f32[2,584,256]{2,1,0:T(8,128)}, f32[2,584,256]{2,1,0:T(8,128)S(1)}, u32[]{:S(2)}, u32[]{:S(2)}) collective-permute-start(f32[2,584,256]{2,1,0:T(8,128)} %get-tuple-element.29), channel_id=1, source_target_pairs={{0,16},{1,17},{2,18},{3,19},{4,20},{5,21},{6,22},{7,23},{8,24},{9,... | collective-permute-start | bytes 3588104 | tf_op jit(solution)/shard_map/ppermute | solution.py:331
  18.3 2.7 %collective-permute-done = f32[2,584,256]{2,1,0:T(8,128)S(1)} collective-permute-done((f32[2,584,256]{2,1,0:T(8,128)}, f32[2,584,256]{2,1,0:T(8,128)S(1)}, u32[]{:S(2)}, u32[]{:S(2)}) %collective-permute-start) | collective-permute-done | bytes 1196064 | tf_op jit(solution)/shard_map/ppermute | solution.py:331
  21.0 1.4 %add.94 = f32[2,584,256]{2,1,0:T(8,128)S(1)} add(f32[2,584,256]{2,1,0:T(8,128)} %get-tuple-element.28, f32[2,584,256]{2,1,0:T(8,128)S(1)} %collective-permute-done) | non-fusion elementwise | flops 299008 | bytes 3588096 | tf_op jit(solution)/shard_map/add | solution.py:369
  22.4 0.0 copy-start.1
  22.5 0.5 collective-permute-start.1
  22.9 1.1 %slice_bitcast_fusion = (f32[584,256]{1,0:T(8,128)}, f32[584,256]{1,0:T(8,128)}) fusion(f32[2,584,256]{2,1,0:T(8,128)S(1)} %add.94), kind=kLoop, calls=%fused_computation.1 | loop fusion | bytes 2392064 | tf_op jit(solution)/shard_map/squeeze | solution.py:371
  24.1 0.0 collective-permute-start.3
  24.1 1.5 %collective-permute-start.2 = (f32[584,256]{1,0:T(8,128)}, f32[584,256]{1,0:T(8,128)}, u32[]{:S(2)}, u32[]{:S(2)}) collective-permute-start(f32[584,256]{1,0:T(8,128)} %get-tuple-element.50), channel_id=1, source_target_pairs={{0,3},{1,2},{2,1},{3,0},{4,7},{5,6},{6,5},{7,4},{8,11},{9,10},{10,... | collective-permute-start | bytes 1794056 | tf_op jit(solution)/shard_map/ppermute | solution.py:331
  25.5 1.8 %collective-permute-start.4 = (f32[72,256]{1,0:T(8,128)S(1)}, f32[72,256]{1,0:T(8,128)S(1)}, u32[]{:S(2)}, u32[]{:S(2)}) collective-permute-start(f32[72,256]{1,0:T(8,128)S(1)} %slice_bitcast_fusion.4), channel_id=1, source_target_pairs={{0,2},{1,3},{2,0},{3,1},{4,6},{5,7},{6,4},{7,5},{8,10},{9,11},{10,... | collective-permute-start | bytes 221192 | tf_op jit(solution)/shard_map/ppermute | solution.py:331
  27.3 0.0 collective-permute-done.1
  27.3 0.0 copy-done.1
  27.3 1.4 %add.95 = f32[2,584,256]{2,1,0:T(8,128)S(1)} add(f32[2,584,256]{2,1,0:T(8,128)S(1)} %copy-done.1, f32[2,584,256]{2,1,0:T(8,128)} %collective-permute-done.1) | non-fusion elementwise | flops 299008 | bytes 3588096 | tf_op jit(solution)/shard_map/add | solution.py:370
  28.8 4.7 %collective-permute-done.3 = f32[584,256]{1,0:T(8,128)S(1)} collective-permute-done((f32[584,256]{1,0:T(8,128)}, f32[584,256]{1,0:T(8,128)S(1)}, u32[]{:S(2)}, u32[]{:S(2)}) %collective-permute-start.3) | collective-permute-done | bytes 598048 | tf_op jit(solution)/shard_map/ppermute | solution.py:331
  33.5 2.0 %collective-permute-done.2 = f32[584,256]{1,0:T(8,128)} collective-permute-done((f32[584,256]{1,0:T(8,128)}, f32[584,256]{1,0:T(8,128)}, u32[]{:S(2)}, u32[]{:S(2)}) %collective-permute-start.2) | collective-permute-done | bytes 598048 | tf_op jit(solution)/shard_map/ppermute | solution.py:331
  35.5 1.2 %fusion = (f32[584,256]{1,0:T(8,128)S(1)}, f32[584,256]{1,0:T(8,128)S(1)}) fusion(f32[584,256]{1,0:T(8,128)S(1)} %collective-permute-done.3, f32[2,584,256]{2,1,0:T(8,128)S(1)} %add.95, f32[584,256]{1,0:T(8,128)} %collective-permute-done.2), kind=kLoop, calls=%fused_computation.3 | loop fusion | flops 299008 | bytes 3588096 | tf_op jit(solution)/shard_map/add | solution.py:371
  36.9 0.0 collective-permute-done.4
  36.9 1.4 %collective-permute-start.5 = (f32[328,256]{1,0:T(8,128)S(1)}, f32[328,256]{1,0:T(8,128)S(1)}, u32[]{:S(2)}, u32[]{:S(2)}) collective-permute-start(f32[328,256]{1,0:T(8,128)S(1)} %get-tuple-element.54), channel_id=1, source_target_pairs={{0,12},{1,13},{2,14},{3,15},{4,8},{5,9},{6,10},{7,11},{8,4},{9,5},... | collective-permute-start | bytes 1007624 | tf_op jit(solution)/shard_map/ppermute | solution.py:331
  38.3 0.0 collective-permute-start.6
  38.3 2.6 %collective-permute-start.10 = (f32[72,256]{1,0:T(8,128)S(1)}, f32[72,256]{1,0:T(8,128)S(1)}, u32[]{:S(2)}, u32[]{:S(2)}) collective-permute-start(f32[72,256]{1,0:T(8,128)S(1)} %fusion.3), channel_id=1, source_target_pairs={{0,8},{1,9},{2,10},{3,11},{4,12},{5,13},{6,14},{7,15},{8,0},{9,1},... | collective-permute-start | bytes 221192 | tf_op jit(solution)/shard_map/ppermute | solution.py:331
  40.9 3.7 %collective-permute-done.5 = f32[328,256]{1,0:T(8,128)S(1)} collective-permute-done((f32[328,256]{1,0:T(8,128)S(1)}, f32[328,256]{1,0:T(8,128)S(1)}, u32[]{:S(2)}, u32[]{:S(2)}) %collective-permute-start.5) | collective-permute-done | bytes 335904 | tf_op jit(solution)/shard_map/ppermute | solution.py:331
  44.6 0.0 collective-permute-done.6
  44.6 0.1 broadcast_select_fusion
  44.7 2.3 %collective-permute-start.7 = (f32[2,128,256]{2,1,0:T(8,128)S(1)}, f32[2,128,256]{2,1,0:T(8,128)S(1)}, u32[]{:S(2)}, u32[]{:S(2)}) collective-permute-start(f32[2,128,256]{2,1,0:T(8,128)S(1)} %broadcast_select_fusion), channel_id=1, source_target_pairs={{0,2},{1,3},{2,0},{3,1},{4,6},{5,7},{6,4},{7,5},{8,10},{9,11},{10,... | collective-permute-start | bytes 786440 | tf_op jit(solution)/shard_map/ppermute | solution.py:331
  47.0 0.0 collective-permute-done.10
  47.0 6.1 %collective-permute-start.11 = (f32[72,256]{1,0:T(8,128)S(1)}, f32[72,256]{1,0:T(8,128)S(1)}, u32[]{:S(2)}, u32[]{:S(2)}) collective-permute-start(f32[72,256]{1,0:T(8,128)S(1)} %fusion.2), channel_id=1, source_target_pairs={{0,192},{1,193},{2,194},{3,195},{4,196},{5,197},{6,198},{7,199},{8... | collective-permute-start | bytes 221192 | tf_op jit(solution)/shard_map/ppermute | solution.py:331
  53.1 0.0 collective-permute-done.7
  53.1 0.1 select_add_fusion
  53.3 0.5 collective-permute-start.8
  53.8 1.4 %collective-permute-done.11 = f32[72,256]{1,0:T(8,128)S(1)} collective-permute-done((f32[72,256]{1,0:T(8,128)S(1)}, f32[72,256]{1,0:T(8,128)S(1)}, u32[]{:S(2)}, u32[]{:S(2)}) %collective-permute-start.11) | collective-permute-done | bytes 73760 | tf_op jit(solution)/shard_map/ppermute | solution.py:331
  55.2 1.6 %collective-permute-start.12 = (f32[72,256]{1,0:T(8,128)S(1)}, f32[72,256]{1,0:T(8,128)S(1)}, u32[]{:S(2)}, u32[]{:S(2)}) collective-permute-start(f32[72,256]{1,0:T(8,128)S(1)} %add.113), channel_id=1, source_target_pairs={{0,64},{1,65},{2,66},{3,67},{4,68},{5,69},{6,70},{7,71},{8,72},{9,... | collective-permute-start | bytes 221192 | tf_op jit(solution)/shard_map/ppermute | solution.py:331
  56.8 2.3 %collective-permute-done.12 = f32[72,256]{1,0:T(8,128)S(1)} collective-permute-done((f32[72,256]{1,0:T(8,128)S(1)}, f32[72,256]{1,0:T(8,128)S(1)}, u32[]{:S(2)}, u32[]{:S(2)}) %collective-permute-start.12) | collective-permute-done | bytes 73760 | tf_op jit(solution)/shard_map/ppermute | solution.py:331
  59.1 0.0 collective-permute-done.8
  59.2 1.0 %collective-permute-start.13 = (f32[72,256]{1,0:T(8,128)S(1)}, f32[72,256]{1,0:T(8,128)S(1)}, u32[]{:S(2)}, u32[]{:S(2)}) collective-permute-start(f32[72,256]{1,0:T(8,128)S(1)} %add.114), channel_id=1, source_target_pairs={{0,32},{1,33},{2,34},{3,35},{4,36},{5,37},{6,38},{7,39},{8,40},{9,... | collective-permute-start | bytes 221192 | tf_op jit(solution)/shard_map/ppermute | solution.py:331
  60.2 1.4 %collective-permute-start.9 = (f32[128,256]{1,0:T(8,128)S(1)}, f32[128,256]{1,0:T(8,128)S(1)}, u32[]{:S(2)}, u32[]{:S(2)}) collective-permute-start(f32[128,256]{1,0:T(8,128)S(1)} %bitcast_add_fusion.2), channel_id=1, source_target_pairs={{0,32},{1,33},{2,34},{3,35},{4,36},{5,37},{6,38},{7,39},{8,40},{9,... | collective-permute-start | bytes 393224 | tf_op jit(solution)/shard_map/ppermute | solution.py:331
  61.6 5.5 %collective-permute-done.13 = f32[72,256]{1,0:T(8,128)S(1)} collective-permute-done((f32[72,256]{1,0:T(8,128)S(1)}, f32[72,256]{1,0:T(8,128)S(1)}, u32[]{:S(2)}, u32[]{:S(2)}) %collective-permute-start.13) | collective-permute-done | bytes 73760 | tf_op jit(solution)/shard_map/ppermute | solution.py:331
  67.1 5.0 %collective-permute-start.14 = (f32[72,256]{1,0:T(8,128)S(1)}, f32[72,256]{1,0:T(8,128)S(1)}, u32[]{:S(2)}, u32[]{:S(2)}) collective-permute-start(f32[72,256]{1,0:T(8,128)S(1)} %add.115), channel_id=1, source_target_pairs={{0,16},{1,17},{2,18},{3,19},{4,20},{5,21},{6,22},{7,23},{8,24},{9,... | collective-permute-start | bytes 221192 | tf_op jit(solution)/shard_map/ppermute | solution.py:331
  72.1 0.0 collective-permute-done.9
  72.1 0.9 collective-permute-done.14
  73.0 0.1 collective-permute-start.15
  73.1 5.2 %factorize_first.1 = (f32[256,256]{1,0:T(8,128)S(1)}, f32[256,128]{1,0:T(8,128)S(1)}, f32[8,256]{1,0:T(8,128)S(1)}) custom-call(f32[72,256]{1,0:T(8,128)S(1)} %get-tuple-element.33.corner_ref, f32[72,256]{1,0:T(8,128)S(1)} %get-tuple-element.34.mixed_ref), custom_call_target="tpu_custom_call" | custom-call | flops 6442450944 | bytes 1048576 | tf_op jit(solution)/shard_map/factorize_first/pallas_call | solution.py:285
  78.3 0.0 collective-permute-done.15
  78.3 0.0 copy-start
  78.3 5.6 %collective-permute-start.16 = (f32[128,256]{1,0:T(8,128)S(1)}, f32[128,256]{1,0:T(8,128)S(1)}, u32[]{:S(2)}, u32[]{:S(2)}) collective-permute-start(f32[128,256]{1,0:T(8,128)S(1)} %add.116), channel_id=1, source_target_pairs={{0,192},{1,193},{2,194},{3,195},{4,196},{5,197},{6,198},{7,199},{8... | collective-permute-start | bytes 393224 | tf_op jit(solution)/shard_map/ppermute | solution.py:331
  83.9 4.8 %factorize_second.1 = (f32[256,256]{1,0:T(8,128)}, f32[256,256]{1,0:T(8,128)S(1)}) custom-call(f32[256,256]{1,0:T(8,128)S(1)} %get-tuple-element.39.state_ref, f32[256,128]{1,0:T(8,128)S(1)} %get-tuple-element.40.upper_ref, f32[8,256]{1,0:T(8,128)S(1)} %get-tuple-element.41.scales_ref), custom_call_target="tpu_custom_call" | custom-call | flops 6442450944 | bytes 1048576 | tf_op jit(solution)/shard_map/factorize_second/pallas_call | solution.py:300
  88.7 0.3 collective-permute-done.16
  89.1 1.2 %collective-permute-start.17 = (f32[128,256]{1,0:T(8,128)S(1)}, f32[128,256]{1,0:T(8,128)S(1)}, u32[]{:S(2)}, u32[]{:S(2)}) collective-permute-start(f32[128,256]{1,0:T(8,128)S(1)} %add.117), channel_id=1, source_target_pairs={{0,16},{1,17},{2,18},{3,19},{4,20},{5,21},{6,22},{7,23},{8,24},{9,... | collective-permute-start | bytes 393224 | tf_op jit(solution)/shard_map/ppermute | solution.py:331
  90.3 0.0 copy-done
  90.3 1.8 %basis.1 = bf16[1024,256]{1,0:T(8,128)(2,1)} custom-call(f32[1024,256]{1,0:T(8,128)S(1)} %copy-done, f32[256,256]{1,0:T(8,128)S(1)} %get-tuple-element.44.inverse_ref), custom_call_target="tpu_custom_call" | custom-call | flops 2147483648 | bytes 1048576 | tf_op jit(solution)/shard_map/basis/pallas_call | solution.py:315
  92.1 0.0 collective-permute-done.17
  92.1 0.8 convolution_multiply_fusion
  (19 shorter events, 0.4 us)
Async XLA Ops:
  15.0 6.0 %collective-permute-start = (f32[2,584,256]{2,1,0:T(8,128)}, f32[2,584,256]{2,1,0:T(8,128)S(1)}, u32[]{:S(2)}, u32[]{:S(2)}) collective-permute-start(f32[2,584,256]{2,1,0:T(8,128)} %get-tuple-element.29), channel_id=1, source_target_pairs={{0,16},{1,17},{2,18},{3,19},{4,20},{5,21},{6,22},{7,23},{8,24},{9,... | collective-permute-start | bytes 3588104 | tf_op jit(solution)/shard_map/ppermute | solution.py:331
  22.4 4.9 %copy-start.1 = (f32[2,584,256]{2,1,0:T(8,128)S(1)}, f32[2,584,256]{2,1,0:T(8,128)}, u32[]{:S(2)}) copy-start(f32[2,584,256]{2,1,0:T(8,128)} %get-tuple-element.26) | copy-start | bytes 3588100
  22.5 4.9 %collective-permute-start.1 = (f32[2,584,256]{2,1,0:T(8,128)}, f32[2,584,256]{2,1,0:T(8,128)}, u32[]{:S(2)}, u32[]{:S(2)}) collective-permute-start(f32[2,584,256]{2,1,0:T(8,128)} %get-tuple-element.30), channel_id=1, source_target_pairs={{0,16},{1,17},{2,18},{3,19},{4,20},{5,21},{6,22},{7,23},{8,24},{9,... | collective-permute-start | bytes 3588104 | tf_op jit(solution)/shard_map/ppermute | solution.py:331
  24.1 9.4 %collective-permute-start.3 = (f32[584,256]{1,0:T(8,128)}, f32[584,256]{1,0:T(8,128)S(1)}, u32[]{:S(2)}, u32[]{:S(2)}) collective-permute-start(f32[584,256]{1,0:T(8,128)} %get-tuple-element.49), channel_id=1, source_target_pairs={{0,1},{1,0},{2,3},{3,2},{4,5},{5,4},{6,7},{7,6},{8,9},{9,8},{10,11... | collective-permute-start | bytes 1794056 | tf_op jit(solution)/shard_map/ppermute | solution.py:331
  24.1 11.4 %collective-permute-start.2 = (f32[584,256]{1,0:T(8,128)}, f32[584,256]{1,0:T(8,128)}, u32[]{:S(2)}, u32[]{:S(2)}) collective-permute-start(f32[584,256]{1,0:T(8,128)} %get-tuple-element.50), channel_id=1, source_target_pairs={{0,3},{1,2},{2,1},{3,0},{4,7},{5,6},{6,5},{7,4},{8,11},{9,10},{10,... | collective-permute-start | bytes 1794056 | tf_op jit(solution)/shard_map/ppermute | solution.py:331
  25.5 11.3 %collective-permute-start.4 = (f32[72,256]{1,0:T(8,128)S(1)}, f32[72,256]{1,0:T(8,128)S(1)}, u32[]{:S(2)}, u32[]{:S(2)}) collective-permute-start(f32[72,256]{1,0:T(8,128)S(1)} %slice_bitcast_fusion.4), channel_id=1, source_target_pairs={{0,2},{1,3},{2,0},{3,1},{4,6},{5,7},{6,4},{7,5},{8,10},{9,11},{10,... | collective-permute-start | bytes 221192 | tf_op jit(solution)/shard_map/ppermute | solution.py:331
  36.9 7.6 %collective-permute-start.5 = (f32[328,256]{1,0:T(8,128)S(1)}, f32[328,256]{1,0:T(8,128)S(1)}, u32[]{:S(2)}, u32[]{:S(2)}) collective-permute-start(f32[328,256]{1,0:T(8,128)S(1)} %get-tuple-element.54), channel_id=1, source_target_pairs={{0,12},{1,13},{2,14},{3,15},{4,8},{5,9},{6,10},{7,11},{8,4},{9,5},... | collective-permute-start | bytes 1007624 | tf_op jit(solution)/shard_map/ppermute | solution.py:331
  38.3 6.3 %collective-permute-start.6 = (f32[328,256]{1,0:T(8,128)S(1)}, f32[328,256]{1,0:T(8,128)S(1)}, u32[]{:S(2)}, u32[]{:S(2)}) collective-permute-start(f32[328,256]{1,0:T(8,128)S(1)} %get-tuple-element.53), channel_id=1, source_target_pairs={{0,4},{1,5},{2,6},{3,7},{4,0},{5,1},{6,2},{7,3},{8,12},{9,13},{10,... | collective-permute-start | bytes 1007624 | tf_op jit(solution)/shard_map/ppermute | solution.py:331
  38.3 8.7 %collective-permute-start.10 = (f32[72,256]{1,0:T(8,128)S(1)}, f32[72,256]{1,0:T(8,128)S(1)}, u32[]{:S(2)}, u32[]{:S(2)}) collective-permute-start(f32[72,256]{1,0:T(8,128)S(1)} %fusion.3), channel_id=1, source_target_pairs={{0,8},{1,9},{2,10},{3,11},{4,12},{5,13},{6,14},{7,15},{8,0},{9,1},... | collective-permute-start | bytes 221192 | tf_op jit(solution)/shard_map/ppermute | solution.py:331
  44.7 8.4 %collective-permute-start.7 = (f32[2,128,256]{2,1,0:T(8,128)S(1)}, f32[2,128,256]{2,1,0:T(8,128)S(1)}, u32[]{:S(2)}, u32[]{:S(2)}) collective-permute-start(f32[2,128,256]{2,1,0:T(8,128)S(1)} %broadcast_select_fusion), channel_id=1, source_target_pairs={{0,2},{1,3},{2,0},{3,1},{4,6},{5,7},{6,4},{7,5},{8,10},{9,11},{10,... | collective-permute-start | bytes 786440 | tf_op jit(solution)/shard_map/ppermute | solution.py:331
  47.0 8.2 %collective-permute-start.11 = (f32[72,256]{1,0:T(8,128)S(1)}, f32[72,256]{1,0:T(8,128)S(1)}, u32[]{:S(2)}, u32[]{:S(2)}) collective-permute-start(f32[72,256]{1,0:T(8,128)S(1)} %fusion.2), channel_id=1, source_target_pairs={{0,192},{1,193},{2,194},{3,195},{4,196},{5,197},{6,198},{7,199},{8... | collective-permute-start | bytes 221192 | tf_op jit(solution)/shard_map/ppermute | solution.py:331
  53.3 5.9 %collective-permute-start.8 = (f32[128,256]{1,0:T(8,128)S(1)}, f32[128,256]{1,0:T(8,128)S(1)}, u32[]{:S(2)}, u32[]{:S(2)}) collective-permute-start(f32[128,256]{1,0:T(8,128)S(1)} %dynamic-slice_bitcast_fusion), channel_id=1, source_target_pairs={{0,8},{1,9},{2,10},{3,11},{4,12},{5,13},{6,14},{7,15},{8,0},{9,1},... | collective-permute-start | bytes 393224 | tf_op jit(solution)/shard_map/ppermute | solution.py:331
  55.2 3.9 %collective-permute-start.12 = (f32[72,256]{1,0:T(8,128)S(1)}, f32[72,256]{1,0:T(8,128)S(1)}, u32[]{:S(2)}, u32[]{:S(2)}) collective-permute-start(f32[72,256]{1,0:T(8,128)S(1)} %add.113), channel_id=1, source_target_pairs={{0,64},{1,65},{2,66},{3,67},{4,68},{5,69},{6,70},{7,71},{8,72},{9,... | collective-permute-start | bytes 221192 | tf_op jit(solution)/shard_map/ppermute | solution.py:331
  59.2 7.9 %collective-permute-start.13 = (f32[72,256]{1,0:T(8,128)S(1)}, f32[72,256]{1,0:T(8,128)S(1)}, u32[]{:S(2)}, u32[]{:S(2)}) collective-permute-start(f32[72,256]{1,0:T(8,128)S(1)} %add.114), channel_id=1, source_target_pairs={{0,32},{1,33},{2,34},{3,35},{4,36},{5,37},{6,38},{7,39},{8,40},{9,... | collective-permute-start | bytes 221192 | tf_op jit(solution)/shard_map/ppermute | solution.py:331
  60.2 11.9 %collective-permute-start.9 = (f32[128,256]{1,0:T(8,128)S(1)}, f32[128,256]{1,0:T(8,128)S(1)}, u32[]{:S(2)}, u32[]{:S(2)}) collective-permute-start(f32[128,256]{1,0:T(8,128)S(1)} %bitcast_add_fusion.2), channel_id=1, source_target_pairs={{0,32},{1,33},{2,34},{3,35},{4,36},{5,37},{6,38},{7,39},{8,40},{9,... | collective-permute-start | bytes 393224 | tf_op jit(solution)/shard_map/ppermute | solution.py:331
  67.1 5.9 %collective-permute-start.14 = (f32[72,256]{1,0:T(8,128)S(1)}, f32[72,256]{1,0:T(8,128)S(1)}, u32[]{:S(2)}, u32[]{:S(2)}) collective-permute-start(f32[72,256]{1,0:T(8,128)S(1)} %add.115), channel_id=1, source_target_pairs={{0,16},{1,17},{2,18},{3,19},{4,20},{5,21},{6,22},{7,23},{8,24},{9,... | collective-permute-start | bytes 221192 | tf_op jit(solution)/shard_map/ppermute | solution.py:331
  73.0 5.3 %collective-permute-start.15 = (f32[128,256]{1,0:T(8,128)S(1)}, f32[128,256]{1,0:T(8,128)S(1)}, u32[]{:S(2)}, u32[]{:S(2)}) collective-permute-start(f32[128,256]{1,0:T(8,128)S(1)} %add.109), channel_id=1, source_target_pairs={{0,64},{1,65},{2,66},{3,67},{4,68},{5,69},{6,70},{7,71},{8,72},{9,... | collective-permute-start | bytes 393224 | tf_op jit(solution)/shard_map/ppermute | solution.py:331
  78.3 12.0 %copy-start = (f32[1024,256]{1,0:T(8,128)S(1)}, f32[1024,256]{1,0:T(8,128)}, u32[]{:S(2)}) copy-start(f32[1024,256]{1,0:T(8,128)} %get-tuple-element.25.sketched_ref) | copy-start | bytes 3145732
  78.3 10.7 %collective-permute-start.16 = (f32[128,256]{1,0:T(8,128)S(1)}, f32[128,256]{1,0:T(8,128)S(1)}, u32[]{:S(2)}, u32[]{:S(2)}) collective-permute-start(f32[128,256]{1,0:T(8,128)S(1)} %add.116), channel_id=1, source_target_pairs={{0,192},{1,193},{2,194},{3,195},{4,196},{5,197},{6,198},{7,199},{8... | collective-permute-start | bytes 393224 | tf_op jit(solution)/shard_map/ppermute | solution.py:331
  89.1 3.0 %collective-permute-start.17 = (f32[128,256]{1,0:T(8,128)S(1)}, f32[128,256]{1,0:T(8,128)S(1)}, u32[]{:S(2)}, u32[]{:S(2)}) collective-permute-start(f32[128,256]{1,0:T(8,128)S(1)} %add.117), channel_id=1, source_target_pairs={{0,16},{1,17},{2,18},{3,19},{4,20},{5,21},{6,22},{7,23},{8,24},{9,... | collective-permute-start | bytes 393224 | tf_op jit(solution)/shard_map/ppermute | solution.py:331
